TPU v7x, 32 devices: a whole 2x2x4 slice. The times are simulated.
32 devices in a mesh: ctx: 8 (over y, x, core), tp: 4 (over z).
Axes of the slice: x: 2, y: 2, z: 4, core: 2. Of those that a mesh axis runs over, the one named last changes fastest.
Arguments:
- query_rows: bfloat16 [4096, 8192], P('ctx', 'tp'), may hold values from -6 to 6
- key_rows: bfloat16 [4096, 8192], P('ctx', 'tp'), may hold values from -6 to 6
- value_rows: bfloat16 [4096, 8192], P('ctx', 'tp'), may hold values from -6 to 6
- positions: int32 [8, 512], replicated, may hold values from -1 to 255, as said below
- filters: float32 [8192, 2048], P(('tp', 'ctx')), may hold values from -6 to 6
- bias_term: float32 [8192], P(('tp', 'ctx')), may hold values from -4 to 4
- grad_out: bfloat16 [2048, 8192], P(('ctx', 'tp')), may hold values from -6 to 6
Outputs:
- output: bfloat16 [2048, 8192], P('ctx', 'tp')
- grad_query: bfloat16 [2048, 8192], P('ctx', 'tp')
- grad_key: bfloat16 [2048, 8192], P('ctx', 'tp')
- grad_value: bfloat16 [2048, 8192], P('ctx', 'tp')
- grad_filters: float32 [8192, 2048], P(('tp', 'ctx'))
Inputs may be any that keep to these rules, and one draw needn't show every extreme that they name: Entries j * 64 to (j + 1) * 64 - 1 of row i list the positions within context shard j of the rows that loader buffer i holds for shard j, or -1 for an unused row; live rows come first in such a slot and carry consecutive positions (one run of a segment). Over all buffers every position of every shard appears exactly once, and for every shard some buffer fills its whole slot of 64 rows.
All inputs are finite; a program needn't handle non-finite values.
Results may differ from a plain program's by a relative error of at most 0.0058.
Values may be sent and summed in bfloat16 or wider, within the bound.
No kernel may reach another device: no remote copies, remote signals or barrier semaphores. Data moves between devices by JAX's collectives and lax.ppermute only.
A program may use at most 128 MiB of HBM per device.

v0:
```python
import math

import jax
import jax.numpy as jnp
from jax import lax
from jax.sharding import PartitionSpec as P

PRECISE = lax.Precision.HIGH


def settle_rows(rows, target, length):
    empty = jnp.zeros((length, rows.shape[1]), rows.dtype)
    return empty.at[target].set(rows, mode="drop")


def dft_tables(length):
    blocks = length // 128
    row_index = jnp.arange(blocks, dtype=jnp.int32)
    col_index = jnp.arange(128, dtype=jnp.int32)
    angle_rows = (row_index[:, None] * row_index[None, :] % blocks).astype(jnp.float32) * (
        2.0 * math.pi / blocks
    )
    angle_cols = (col_index[:, None] * col_index[None, :] % 128).astype(jnp.float32) * (
        2.0 * math.pi / 128
    )
    angle_twist = (row_index[:, None] * col_index[None, :] % length).astype(jnp.float32) * (
        2.0 * math.pi / length
    )
    return (
        jnp.cos(angle_rows),
        jnp.sin(angle_rows),
        jnp.cos(angle_cols),
        jnp.sin(angle_cols),
        jnp.cos(angle_twist),
        jnp.sin(angle_twist),
    )


def forward_dft(signal, tables):
    cos_rows, sin_rows, cos_cols, sin_cols, cos_twist, sin_twist = tables
    lower = cos_rows.shape[0] // 2
    grid = signal.reshape(signal.shape[0], lower, 128)
    first_re = jnp.einsum("kn,cns->cks", cos_rows[:, :lower], grid, precision=PRECISE)
    first_im = -jnp.einsum("kn,cns->cks", sin_rows[:, :lower], grid, precision=PRECISE)
    twist_re = first_re * cos_twist + first_im * sin_twist
    twist_im = first_im * cos_twist - first_re * sin_twist
    out_re = jnp.einsum("cks,sj->ckj", twist_re, cos_cols, precision=PRECISE) + jnp.einsum(
        "cks,sj->ckj", twist_im, sin_cols, precision=PRECISE
    )
    out_im = jnp.einsum("cks,sj->ckj", twist_im, cos_cols, precision=PRECISE) - jnp.einsum(
        "cks,sj->ckj", twist_re, sin_cols, precision=PRECISE
    )
    return (out_re, out_im)


def inverse_dft(spec_re, spec_im, tables):
    cos_rows, sin_rows, cos_cols, sin_cols, cos_twist, sin_twist = tables
    blocks = cos_rows.shape[0]
    lower = blocks // 2
    mid_re = jnp.einsum("ckj,js->cks", spec_re, cos_cols, precision=PRECISE) - jnp.einsum(
        "ckj,js->cks", spec_im, sin_cols, precision=PRECISE
    )
    mid_im = jnp.einsum("ckj,js->cks", spec_im, cos_cols, precision=PRECISE) + jnp.einsum(
        "ckj,js->cks", spec_re, sin_cols, precision=PRECISE
    )
    twist_re = mid_re * cos_twist - mid_im * sin_twist
    twist_im = mid_im * cos_twist + mid_re * sin_twist
    rows_out = jnp.einsum(
        "nk,cks->cns", cos_rows[:lower, :], twist_re, precision=PRECISE
    ) - jnp.einsum("nk,cks->cns", sin_rows[:lower, :], twist_im, precision=PRECISE)
    return rows_out.reshape(spec_re.shape[0], lower * 128) * (1.0 / (blocks * 128))


def per_device(query_rows, key_rows, value_rows, positions, filters, bias_term, grad_out):
    ctx_count = lax.axis_size("ctx")
    ctx_index = lax.axis_index("ctx")
    buffer_rows = query_rows.shape[0]
    slot_rows = buffer_rows // ctx_count
    own_tokens = buffer_rows // 2
    seq_length = own_tokens * ctx_count
    factor = 1.0 / math.sqrt(seq_length)
    tables = dft_tables(2 * seq_length)
    grad_tokens = lax.all_to_all(grad_out, "tp", split_axis=1, concat_axis=0, tiled=True)
    own_slots = lax.dynamic_slice_in_dim(positions, ctx_index * slot_rows, slot_rows, 1).reshape(-1)
    own_target = jnp.where(own_slots >= 0, own_slots, own_tokens)
    recv_query, recv_key, recv_value = (
        lax.all_to_all(query_rows, "ctx", split_axis=0, concat_axis=0, tiled=True),
        lax.all_to_all(key_rows, "ctx", split_axis=0, concat_axis=0, tiled=True),
        lax.all_to_all(value_rows, "ctx", split_axis=0, concat_axis=0, tiled=True),
    )
    query_seq = settle_rows(recv_query, own_target, own_tokens)
    key_seq = settle_rows(recv_key, own_target, own_tokens)
    value_seq = settle_rows(recv_value, own_target, own_tokens)
    signal_seq = (key_seq.astype(jnp.float32) * value_seq.astype(jnp.float32)).astype(jnp.bfloat16)
    grad_conv = (grad_tokens.astype(jnp.float32) * query_seq.astype(jnp.float32)).astype(
        jnp.bfloat16
    )
    signal_chan, grad_chan = (
        lax.all_to_all(signal_seq.T, "ctx", split_axis=0, concat_axis=1, tiled=True),
        lax.all_to_all(grad_conv.T, "ctx", split_axis=0, concat_axis=1, tiled=True),
    )
    signal_wide = signal_chan.astype(jnp.float32)
    grad_wide = grad_chan.astype(jnp.float32)
    signal_re, signal_im = forward_dft(signal_wide, tables)
    filter_re, filter_im = forward_dft(filters, tables)
    grad_re, grad_im = forward_dft(grad_wide, tables)
    forward_conv = inverse_dft(
        filter_re * signal_re - filter_im * signal_im,
        filter_re * signal_im + filter_im * signal_re,
        tables,
    )
    backward_conv = inverse_dft(
        filter_re * grad_re + filter_im * grad_im, filter_re * grad_im - filter_im * grad_re, tables
    )
    filter_corr = inverse_dft(
        signal_re * grad_re + signal_im * grad_im, signal_re * grad_im - signal_im * grad_re, tables
    )
    conv_out = (bias_term[:, None] * signal_wide + factor * forward_conv).astype(jnp.bfloat16)
    grad_signal = (bias_term[:, None] * grad_wide + factor * backward_conv).astype(jnp.bfloat16)
    grad_filters = factor * filter_corr
    conv_back, signal_back = (
        lax.all_to_all(conv_out, "ctx", split_axis=1, concat_axis=0, tiled=True),
        lax.all_to_all(grad_signal, "ctx", split_axis=1, concat_axis=0, tiled=True),
    )
    conv_seq = conv_back.T
    grad_signal_seq = signal_back.T.astype(jnp.float32)
    grad_key = (grad_signal_seq * value_seq.astype(jnp.float32)).astype(jnp.bfloat16)
    grad_value = (grad_signal_seq * key_seq.astype(jnp.float32)).astype(jnp.bfloat16)
    conv_float = conv_seq.astype(jnp.float32)
    output = (query_seq.astype(jnp.float32) * conv_float).astype(jnp.bfloat16)
    grad_query = (grad_tokens.astype(jnp.float32) * conv_float).astype(jnp.bfloat16)
    return (output, grad_query, grad_key, grad_value, grad_filters)


def solution(mesh):
    in_specs = (
        P("ctx", "tp"),
        P("ctx", "tp"),
        P("ctx", "tp"),
        P(),
        P(("tp", "ctx"), None),
        P(("tp", "ctx")),
        P(("ctx", "tp"), None),
    )
    out_specs = (
        P("ctx", "tp"),
        P("ctx", "tp"),
        P("ctx", "tp"),
        P("ctx", "tp"),
        P(("tp", "ctx"), None),
    )
    return jax.shard_map(
        per_device, mesh=mesh, in_specs=in_specs, out_specs=out_specs, check_vma=False
    )
```

profile of v0, /device:TPU:0, one launch (start us, length us, event | category | flops | bytes accessed | tf_op | source)
XLA Modules:
  0.0 360.2 jit_solution(8550913907030877152)
XLA Ops:
  2.1 31.8 %all_to_all.101 = bf16[64,4,2048]{2,0,1:T(8,128)(2,1)S(1)} all-to-all(bf16[64,4,2048]{2,0,1:T(8,128)(2,1)S(1)} %bitcast.181), channel_id=1, replica_groups=mesh['ctx'=8,'tp'=4] {'tp'}, dimensions={1} | all-to-all | bytes 2097152 | tf_op jit(solution)/shard_map/all_to_all | solution.py:83
  34.0 30.2 %all_to_all.102 = bf16[8,64,2048]{2,1,0:T(8,128)(2,1)} all-to-all(bf16[8,64,2048]{2,1,0:T(8,128)(2,1)S(1)} %bitcast.182), channel_id=1, replica_groups=mesh['ctx'=8,'tp'=4] {'ctx'}, dimensions={0} | all-to-all | bytes 4194304 | tf_op jit(solution)/shard_map/all_to_all | solution.py:88
  64.2 4.4 %all-to-all-start.2 = ((bf16[8,64,2048]{2,1,0:T(8,128)(2,1)}), bf16[8,64,2048]{2,1,0:T(8,128)(2,1)}, u32[]{:S(2)}, u32[]{:S(2)}) async-start(bf16[8,64,2048]{2,1,0:T(8,128)(2,1)} %bitcast.5), calls=%async_computation.2 | async-start | bytes 4194304 | tf_op jit(solution)/shard_map/all_to_all | solution.py:89
  72.6 4.9 %add_bitcast_fusion = (f32[256,32,128]{2,1,0:T(8,128)}, f32[256,32,128]{2,1,0:T(8,128)}) fusion(f32[32,256,128]{2,0,1:T(8,128)S(1)} %fusion.219, f32[32,128]{1,0:T(8,128)S(1)} %get-tuple-element.29, f32[32,128]{1,0:T(8,128)S(1)} %get-tuple-element.30, f32[256,16,128]{2,1,0:T(8,128)S(1)} %bitcast.172, f32[32,32]{0,1:T(8,128)S(1)} %fusion.215), kind=kOutput, calls=%fused_computation.46 | convolution fusion | flops 108003328 | bytes 14721024 | tf_op jit(solution)/shard_map/kn,cns->cks/dot_general | solution.py:44
  77.6 17.6 %all-to-all-done.2 = bf16[8,64,2048]{2,1,0:T(8,128)(2,1)} async-done(((bf16[8,64,2048]{2,1,0:T(8,128)(2,1)}), bf16[8,64,2048]{2,1,0:T(8,128)(2,1)}, u32[]{:S(2)}, u32[]{:S(2)}) %all-to-all-start.2) | async-done | bytes 2097184 | tf_op jit(solution)/shard_map/all_to_all | solution.py:89
  95.2 4.5 %all-to-all-start = ((bf16[8,64,2048]{2,1,0:T(8,128)(2,1)}), bf16[8,64,2048]{2,1,0:T(8,128)(2,1)}, u32[]{:S(2)}, u32[]{:S(2)}) async-start(bf16[8,64,2048]{2,1,0:T(8,128)(2,1)} %bitcast.184), calls=%async_computation | async-start | bytes 4194304 | tf_op jit(solution)/shard_map/all_to_all | solution.py:87
  99.9 6.8 %fusion.70 = f32[256,32,128]{2,0,1:T(8,128)S(1)} fusion(f32[256,32,128]{2,1,0:T(8,128)} %get-tuple-element.16), kind=kOutput, calls=%fused_computation.89 | convolution fusion | flops 805535744 | bytes 8388608 | tf_op jit(solution)/shard_map/cks,sj->ckj/dot_general | solution.py:47
  106.8 5.7 %fusion.76 = f32[256,32,128]{2,0,1:T(8,128)} fusion(f32[256,32,128]{2,0,1:T(8,128)S(1)} %fusion.70, f32[256,32,128]{2,1,0:T(8,128)S(1)} %copy-done.2), kind=kOutput, calls=%fused_computation.100 | convolution fusion | flops 806584320 | bytes 12582912 | tf_op jit(solution)/shard_map/cks,sj->ckj/dot_general | solution.py:47
  112.4 4.8 %scatter_custom_fusion.1 = bf16[256,2048]{1,0:T(8,128)(2,1)S(1)} fusion(s32[512]{0:T(512)S(1)} %bitcast.188, bf16[512,2048]{1,0:T(8,128)(2,1)} %bitcast.185, bf16[]{:T(256)} %constant.55.clone.1), kind=kCustom, calls=%fused_computation.143 | custom fusion | bytes 1049088 | tf_op jit(solution)/shard_map/scatter | solution.py:13
  117.3 5.3 %scatter_custom_fusion.2 = bf16[256,2048]{1,0:T(8,128)(2,1)S(1)} fusion(s32[512]{0:T(512)S(1)} %bitcast.189, bf16[512,2048]{1,0:T(8,128)(2,1)} %bitcast.6, bf16[]{:T(256)} %constant.55.clone.1), kind=kCustom, calls=%fused_computation.141 | custom fusion | bytes 1049088 | tf_op jit(solution)/shard_map/scatter | solution.py:13
  126.4 3.9 %all-to-all-start.3 = ((bf16[8,256,256]{2,1,0:T(8,128)(2,1)}), bf16[8,256,256]{2,1,0:T(8,128)(2,1)S(1)}, u32[]{:S(2)}, u32[]{:S(2)}) async-start(bf16[8,256,256]{2,1,0:T(8,128)(2,1)} %bitcast.180), calls=%async_computation.3 | async-start | bytes 2097152 | tf_op jit(solution)/shard_map/all_to_all | solution.py:99
  130.4 8.3 %fusion.68 = f32[256,32,128]{2,0,1:T(8,128)} fusion(f32[256,32,128]{2,1,0:T(8,128)} %get-tuple-element.16), kind=kOutput, calls=%fused_computation.87 | convolution fusion | flops 805535744 | bytes 8388608 | tf_op jit(solution)/shard_map/cks,sj->ckj/dot_general | solution.py:50
  138.7 4.8 %scatter_custom_fusion = bf16[256,2048]{1,0:T(8,128)(2,1)S(1)} fusion(s32[512]{0:T(512)S(1)} %bitcast.190, bf16[512,2048]{1,0:T(8,128)(2,1)} %bitcast.2, bf16[]{:T(256)} %constant.55.clone.1), kind=kCustom, calls=%fused_computation.145 | custom fusion | bytes 1049088 | tf_op jit(solution)/shard_map/scatter | solution.py:13
  147.2 4.6 %all-to-all-start.6 = ((bf16[8,256,256]{2,1,0:T(8,128)(2,1)}), bf16[8,256,256]{2,1,0:T(8,128)(2,1)S(1)}, u32[]{:S(2)}, u32[]{:S(2)}) async-start(bf16[8,256,256]{2,1,0:T(8,128)(2,1)} %bitcast.179), calls=%async_computation.6 | async-start | bytes 2097152 | tf_op jit(solution)/shard_map/all_to_all | solution.py:100
  151.8 9.6 %fusion.79 = f32[256,32,128]{2,0,1:T(8,128)} fusion(f32[256,32,128]{2,0,1:T(8,128)} %fusion.68, f32[256,32,128]{2,1,0:T(8,128)} %get-tuple-element.15), kind=kOutput, calls=%fused_computation.101 | convolution fusion | flops 806584320 | bytes 12582912 | tf_op jit(solution)/shard_map/cks,sj->ckj/dot_general | solution.py:50
  164.4 3.2 fusion.221
  167.6 3.3 fusion.218
  173.9 3.3 fusion.220
  177.2 5.8 %fusion = (f32[256,32,128]{2,1,0:T(8,128)S(1)}, f32[256,32,128]{2,1,0:T(8,128)S(1)}, f32[256,32,128]{2,1,0:T(8,128)S(1)}, f32[256,32,128]{2,1,0:T(8,128)S(1)}) fusion(f32[256,128,32]{1,2,0:T(8,128)} %fusion.220, f32[32,128]{1,0:T(8,128)S(1)} %get-tuple-element.29, f32[32,128]{1,0:T(8,128)S(1)} %get-tuple-element.30, f32[256,128,32]{1,2,0:T(8,128)} %fusion.218, ...), kind=kOutput, calls=%fused_computation.5 | convolution fusion | flops 115343360 | bytes 30449664 | tf_op jit(solution)/shard_map/kn,cns->cks/dot_general | solution.py:43
  183.0 4.1 %fusion.52 = f32[256,32,128]{2,0,1:T(8,128)S(1)} fusion(f32[256,32,128]{2,1,0:T(8,128)S(1)} %get-tuple-element.12), kind=kOutput, calls=%fused_computation.71 | convolution fusion | flops 805535744 | bytes 8388608 | tf_op jit(solution)/shard_map/cks,sj->ckj/dot_general | solution.py:50
  187.2 4.1 %fusion.54 = f32[256,32,128]{2,0,1:T(8,128)S(1)} fusion(f32[256,32,128]{2,1,0:T(8,128)S(1)} %get-tuple-element.12), kind=kOutput, calls=%fused_computation.73 | convolution fusion | flops 805535744 | bytes 8388608 | tf_op jit(solution)/shard_map/cks,sj->ckj/dot_general | solution.py:47
  191.3 6.1 %fusion.60 = f32[256,32,128]{2,0,1:T(8,128)} fusion(f32[256,32,128]{2,1,0:T(8,128)S(1)} %get-tuple-element.25), kind=kOutput, calls=%fused_computation.79 | convolution fusion | flops 805535744 | bytes 8388608 | tf_op jit(solution)/shard_map/cks,sj->ckj/dot_general | solution.py:50
  197.4 4.2 %fusion.62 = f32[256,32,128]{2,0,1:T(8,128)S(1)} fusion(f32[256,32,128]{2,1,0:T(8,128)S(1)} %get-tuple-element.25), kind=kOutput, calls=%fused_computation.81 | convolution fusion | flops 805535744 | bytes 8388608 | tf_op jit(solution)/shard_map/cks,sj->ckj/dot_general | solution.py:47
  201.6 5.7 %fusion.88 = f32[256,32,128]{2,0,1:T(8,128)} fusion(f32[256,32,128]{2,0,1:T(8,128)S(1)} %fusion.54, f32[256,32,128]{2,1,0:T(8,128)S(1)} %get-tuple-element.11), kind=kOutput, calls=%fused_computation.104 | convolution fusion | flops 806584320 | bytes 12582912 | tf_op jit(solution)/shard_map/cks,sj->ckj/dot_general | solution.py:47
  207.3 5.7 %fusion.91 = f32[256,32,128]{2,0,1:T(8,128)} fusion(f32[256,32,128]{2,0,1:T(8,128)S(1)} %fusion.52, f32[256,32,128]{2,1,0:T(8,128)S(1)} %get-tuple-element.11), kind=kOutput, calls=%fused_computation.105 | convolution fusion | flops 806584320 | bytes 12582912 | tf_op jit(solution)/shard_map/cks,sj->ckj/dot_general | solution.py:50
  212.9 5.7 %fusion.82 = f32[256,32,128]{2,0,1:T(8,128)} fusion(f32[256,32,128]{2,0,1:T(8,128)S(1)} %fusion.62, f32[256,32,128]{2,1,0:T(8,128)S(1)} %get-tuple-element.26), kind=kOutput, calls=%fused_computation.102 | convolution fusion | flops 806584320 | bytes 12582912 | tf_op jit(solution)/shard_map/cks,sj->ckj/dot_general | solution.py:47
  218.6 17.7 %multiply_add_fusion = (f32[256,32,128]{2,0,1:T(8,128)}, f32[256,32,128]{2,0,1:T(8,128)}, f32[256,32,128]{2,0,1:T(8,128)}, f32[256,32,128]{2,0,1:T(8,128)}, f32[256,32,128]{2,0,1:T(8,128)}, /*index=5*/f32[256,32,128]{2,0,1:T(8,128)}) fusion(f32[256,32,128]{2,0,1:T(8,128)} %fusion.91, f32[256,32,128]{2,0,1:T(8,128)} %fusion.82, f32[256,32,128]{2,0,1:T(8,128)} %fusion.88, ...), kind=kOutput, calls=%fused_computation.24 | convolution fusion | flops 825458688 | bytes 54525952 | tf_op jit(solution)/shard_map/cks,sj->ckj/dot_general | solution.py:50
  236.4 7.5 %fusion.36 = f32[256,32,128]{2,1,0:T(8,128)S(1)} fusion(f32[256,32,128]{2,0,1:T(8,128)} %get-tuple-element.17), kind=kOutput, calls=%fused_computation.55 | convolution fusion | flops 805535744 | bytes 8388608 | tf_op jit(solution)/shard_map/ckj,js->cks/dot_general | solution.py:63
  243.9 4.1 %fusion.38 = f32[256,32,128]{2,1,0:T(8,128)S(1)} fusion(f32[256,32,128]{2,0,1:T(8,128)S(1)} %copy-done.12), kind=kOutput, calls=%fused_computation.57 | convolution fusion | flops 805535744 | bytes 8388608 | tf_op jit(solution)/shard_map/ckj,js->cks/dot_general | solution.py:60
  248.1 5.5 %fusion.44 = f32[256,32,128]{2,1,0:T(8,128)} fusion(f32[256,32,128]{2,0,1:T(8,128)S(1)} %copy-done.11), kind=kOutput, calls=%fused_computation.63 | convolution fusion | flops 805535744 | bytes 8388608 | tf_op jit(solution)/shard_map/ckj,js->cks/dot_general | solution.py:63
  253.5 5.5 %fusion.46 = f32[256,32,128]{2,1,0:T(8,128)} fusion(f32[256,32,128]{2,0,1:T(8,128)S(1)} %copy-done.11), kind=kOutput, calls=%fused_computation.65 | convolution fusion | flops 805535744 | bytes 8388608 | tf_op jit(solution)/shard_map/ckj,js->cks/dot_general | solution.py:60
  259.0 5.9 %fusion.28 = f32[256,32,128]{2,1,0:T(8,128)} fusion(f32[256,32,128]{2,0,1:T(8,128)S(1)} %copy-done.9), kind=kOutput, calls=%fused_computation.47 | convolution fusion | flops 805535744 | bytes 8388608 | tf_op jit(solution)/shard_map/ckj,js->cks/dot_general | solution.py:63
  264.9 4.1 %fusion.103 = f32[256,32,128]{2,1,0:T(8,128)S(1)} fusion(f32[256,32,128]{2,1,0:T(8,128)S(1)} %fusion.36, f32[256,32,128]{2,0,1:T(8,128)S(1)} %copy-done.8), kind=kOutput, calls=%fused_computation.109 | convolution fusion | flops 806584320 | bytes 12582912 | tf_op jit(solution)/shard_map/ckj,js->cks/dot_general | solution.py:63
  269.1 4.1 %fusion.100 = f32[256,32,128]{2,1,0:T(8,128)S(1)} fusion(f32[256,32,128]{2,1,0:T(8,128)S(1)} %fusion.38, f32[256,32,128]{2,0,1:T(8,128)S(1)} %copy-done.8), kind=kOutput, calls=%fused_computation.108 | convolution fusion | flops 806584320 | bytes 12582912 | tf_op jit(solution)/shard_map/ckj,js->cks/dot_general | solution.py:60
  277.6 3.0 mul.891
  280.7 7.7 %fusion.97 = f32[256,32,128]{2,1,0:T(8,128)S(1)} fusion(f32[256,32,128]{2,1,0:T(8,128)} %fusion.44, f32[256,32,128]{2,0,1:T(8,128)} %get-tuple-element.20), kind=kOutput, calls=%fused_computation.107 | convolution fusion | flops 806584320 | bytes 12582912 | tf_op jit(solution)/shard_map/ckj,js->cks/dot_general | solution.py:63
  288.4 4.1 %fusion.94 = f32[256,32,128]{2,1,0:T(8,128)S(1)} fusion(f32[256,32,128]{2,1,0:T(8,128)S(1)} %copy-done.14, f32[256,32,128]{2,0,1:T(8,128)S(1)} %copy-done.6), kind=kOutput, calls=%fused_computation.106 | convolution fusion | flops 806584320 | bytes 12582912 | tf_op jit(solution)/shard_map/ckj,js->cks/dot_general | solution.py:60
  294.1 2.9 multiply_bitcast_fusion.1
  297.0 3.0 mul.872
  300.0 5.1 %fusion.118 = (bf16[256,8,256]{2,0,1:T(8,128)(2,1)}, bf16[256,8,256]{2,0,1:T(8,128)(2,1)}) fusion(f32[256,8,256]{2,1,0:T(8,128)} %mul.891, f32[256]{0:T(256)S(1)} %copy-done.27, bf16[8,256,256]{2,1,0:T(8,128)(2,1)S(1)} %all-to-all-done.6, f32[256,8,256]{2,1,0:T(8,128)} %mul.872, bf16[8,256,256]{2,1,0:T(8,128)(2,1)S(1)} %all-to-all-done.3), kind=kLoop, calls=%fused_computation.121 | loop fusion | flops 4194304 | bytes 8389632 | tf_op jit(solution)/shard_map/convert_element_type | solution.py:119
  305.1 4.2 %all-to-all-start.4 = ((bf16[256,8,256]{2,0,1:T(8,128)(2,1)}), bf16[256,8,256]{2,0,1:T(8,128)(2,1)S(1)}, u32[]{:S(2)}, u32[]{:S(2)}) async-start(bf16[256,8,256]{2,0,1:T(8,128)(2,1)} %get-tuple-element.28), calls=%async_computation.4 | async-start | bytes 2097152 | tf_op jit(solution)/shard_map/all_to_all | solution.py:122
  309.3 9.7 %fusion.109 = f32[256,32,128]{2,1,0:T(8,128)} fusion(f32[256,32,128]{2,1,0:T(8,128)} %fusion.28, f32[256,32,128]{2,0,1:T(8,128)} %get-tuple-element.5), kind=kOutput, calls=%fused_computation.111 | convolution fusion | flops 806584320 | bytes 12582912 | tf_op jit(solution)/shard_map/ckj,js->cks/dot_general | solution.py:63
  319.1 4.1 %fusion.30 = f32[256,32,128]{2,1,0:T(8,128)S(1)} fusion(f32[256,32,128]{2,0,1:T(8,128)S(1)} %copy-done.10), kind=kOutput, calls=%fused_computation.49 | convolution fusion | flops 805535744 | bytes 8388608 | tf_op jit(solution)/shard_map/ckj,js->cks/dot_general | solution.py:60
  323.2 5.5 %fusion.106 = f32[256,32,128]{2,1,0:T(8,128)} fusion(f32[256,32,128]{2,1,0:T(8,128)S(1)} %fusion.30, f32[256,32,128]{2,0,1:T(8,128)S(1)} %copy-done.5), kind=kOutput, calls=%fused_computation.110 | convolution fusion | flops 806584320 | bytes 12582912 | tf_op jit(solution)/shard_map/ckj,js->cks/dot_general | solution.py:60
  328.7 4.5 %all-to-all-start.7 = ((bf16[256,8,256]{2,0,1:T(8,128)(2,1)}), bf16[256,8,256]{2,0,1:T(8,128)(2,1)}, u32[]{:S(2)}, u32[]{:S(2)}) async-start(bf16[256,8,256]{2,0,1:T(8,128)(2,1)} %get-tuple-element.27), calls=%async_computation.7 | async-start | bytes 2097152 | tf_op jit(solution)/shard_map/all_to_all | solution.py:123
  333.2 5.1 %fusion.4 = f32[256,128,16]{1,2,0:T(8,128)S(1)} fusion(f32[256,32,128]{2,1,0:T(8,128)} %fusion.106, f32[256,32,128]{2,1,0:T(8,128)} %fusion.109, f32[32,128]{1,0:T(8,128)S(1)} %get-tuple-element.29, f32[32,128]{1,0:T(8,128)S(1)} %get-tuple-element.30, f32[32,32]{0,1:T(8,128)S(1)} %copy-done.26), kind=kOutput, calls=%fused_computation.15 | convolution fusion | flops 103809024 | bytes 10522624 | tf_op jit(solution)/shard_map/nk,cks->cns/dot_general | solution.py:70
  345.0 3.7 %all-to-all-done.7 = bf16[256,8,256]{2,0,1:T(8,128)(2,1)} async-done(((bf16[256,8,256]{2,0,1:T(8,128)(2,1)}), bf16[256,8,256]{2,0,1:T(8,128)(2,1)}, u32[]{:S(2)}, u32[]{:S(2)}) %all-to-all-start.7) | async-done | bytes 1048608 | tf_op jit(solution)/shard_map/all_to_all | solution.py:123
  354.4 3.6 %fusion.114 = (bf16[256,2048]{1,0:T(8,128)(2,1)}, bf16[256,2048]{1,0:T(8,128)(2,1)}) fusion(bf16[256,2048]{1,0:T(8,128)(2,1)S(1)} %copy-done.18, f32[2048,256]{0,1:T(8,128)} %copy.152, bf16[256,2048]{1,0:T(8,128)(2,1)S(1)} %copy-done.20), kind=kLoop, calls=%fused_computation.114 | loop fusion | flops 3145728 | bytes 6291456 | tf_op jit(solution)/shard_map/convert_element_type | solution.py:128
  (87 shorter events, 39.4 us)
Async XLA Ops:
  0.6 99.1 %copy-start = (s32[8,512]{1,0:T(8,128)S(1)}, s32[8,512]{1,0:T(8,128)}, u32[]{:S(2)}) copy-start(s32[8,512]{1,0:T(8,128)} %param.10) | copy-start | bytes 49156
  0.6 33.3 %copy-start.24 = (bf16[512,2048]{1,0:T(8,128)(2,1)S(1)}, bf16[512,2048]{1,0:T(8,128)(2,1)}, u32[]{:S(2)}) copy-start(bf16[512,2048]{1,0:T(8,128)(2,1)} %param.8) | copy-start | bytes 6291460
  33.9 109.5 %copy-start.15 = (bf16[64,4,2048]{2,0,1:T(8,128)(2,1)}, bf16[64,4,2048]{2,0,1:T(8,128)(2,1)S(1)}, u32[]{:S(2)}) copy-start(bf16[64,4,2048]{2,0,1:T(8,128)(2,1)S(1)} %all_to_all.101) | copy-start | bytes 3145732
  64.2 31.0 %all-to-all-start.2 = ((bf16[8,64,2048]{2,1,0:T(8,128)(2,1)}), bf16[8,64,2048]{2,1,0:T(8,128)(2,1)}, u32[]{:S(2)}, u32[]{:S(2)}) async-start(bf16[8,64,2048]{2,1,0:T(8,128)(2,1)} %bitcast.5), calls=%async_computation.2 | async-start | bytes 4194304 | tf_op jit(solution)/shard_map/all_to_all | solution.py:89
  70.7 6.9 %copy-start.25 = (f32[32,32]{0,1:T(8,128)}, f32[32,32]{0,1:T(8,128)S(1)}, u32[]{:S(2)}) copy-start(f32[32,32]{0,1:T(8,128)S(1)} %fusion.215) | copy-start | bytes 12292
  95.2 31.2 %all-to-all-start = ((bf16[8,64,2048]{2,1,0:T(8,128)(2,1)}), bf16[8,64,2048]{2,1,0:T(8,128)(2,1)}, u32[]{:S(2)}, u32[]{:S(2)}) async-start(bf16[8,64,2048]{2,1,0:T(8,128)(2,1)} %bitcast.184), calls=%async_computation | async-start | bytes 4194304 | tf_op jit(solution)/shard_map/all_to_all | solution.py:87
  99.9 6.9 %copy-start.2 = (f32[256,32,128]{2,1,0:T(8,128)S(1)}, f32[256,32,128]{2,1,0:T(8,128)}, u32[]{:S(2)}) copy-start(f32[256,32,128]{2,1,0:T(8,128)} %get-tuple-element.15) | copy-start | bytes 12582916
  117.2 9.2 %copy-start.17 = (bf16[256,2048]{1,0:T(8,128)(2,1)}, bf16[256,2048]{1,0:T(8,128)(2,1)S(1)}, u32[]{:S(2)}) copy-start(bf16[256,2048]{1,0:T(8,128)(2,1)S(1)} %scatter_custom_fusion.1) | copy-start | bytes 3145732
  122.5 3.9 %copy-start.19 = (bf16[256,2048]{1,0:T(8,128)(2,1)}, bf16[256,2048]{1,0:T(8,128)(2,1)S(1)}, u32[]{:S(2)}) copy-start(bf16[256,2048]{1,0:T(8,128)(2,1)S(1)} %scatter_custom_fusion.2) | copy-start | bytes 3145732
  126.4 20.7 %all-to-all-start.3 = ((bf16[8,256,256]{2,1,0:T(8,128)(2,1)}), bf16[8,256,256]{2,1,0:T(8,128)(2,1)S(1)}, u32[]{:S(2)}, u32[]{:S(2)}) async-start(bf16[8,256,256]{2,1,0:T(8,128)(2,1)} %bitcast.180), calls=%async_computation.3 | async-start | bytes 2097152 | tf_op jit(solution)/shard_map/all_to_all | solution.py:99
  143.5 17.9 %copy-start.21 = (bf16[256,2048]{1,0:T(8,128)(2,1)}, bf16[256,2048]{1,0:T(8,128)(2,1)S(1)}, u32[]{:S(2)}) copy-start(bf16[256,2048]{1,0:T(8,128)(2,1)S(1)} %scatter_custom_fusion) | copy-start | bytes 3145732
  147.2 23.8 %all-to-all-start.6 = ((bf16[8,256,256]{2,1,0:T(8,128)(2,1)}), bf16[8,256,256]{2,1,0:T(8,128)(2,1)S(1)}, u32[]{:S(2)}, u32[]{:S(2)}) async-start(bf16[8,256,256]{2,1,0:T(8,128)(2,1)} %bitcast.179), calls=%async_computation.6 | async-start | bytes 2097152 | tf_op jit(solution)/shard_map/all_to_all | solution.py:100
  161.4 3.0 copy-start.26
  173.9 3.3 copy-start.13
  183.0 29.9 %copy-start.7 = (f32[256,32,128]{2,1,0:T(8,128)}, f32[256,32,128]{2,1,0:T(8,128)S(1)}, u32[]{:S(2)}) copy-start(f32[256,32,128]{2,1,0:T(8,128)S(1)} %get-tuple-element.26) | copy-start | bytes 12582916
  236.4 7.6 %copy-start.12 = (f32[256,32,128]{2,0,1:T(8,128)S(1)}, f32[256,32,128]{2,0,1:T(8,128)}, u32[]{:S(2)}) copy-start(f32[256,32,128]{2,0,1:T(8,128)} %get-tuple-element.17) | copy-start | bytes 12582916
  243.9 4.2 %copy-start.11 = (f32[256,32,128]{2,0,1:T(8,128)S(1)}, f32[256,32,128]{2,0,1:T(8,128)}, u32[]{:S(2)}) copy-start(f32[256,32,128]{2,0,1:T(8,128)} %get-tuple-element.19) | copy-start | bytes 12582916
  253.5 5.5 %copy-start.9 = (f32[256,32,128]{2,0,1:T(8,128)S(1)}, f32[256,32,128]{2,0,1:T(8,128)}, u32[]{:S(2)}) copy-start(f32[256,32,128]{2,0,1:T(8,128)} %get-tuple-element.6) | copy-start | bytes 12582916
  259.0 5.9 %copy-start.8 = (f32[256,32,128]{2,0,1:T(8,128)S(1)}, f32[256,32,128]{2,0,1:T(8,128)}, u32[]{:S(2)}) copy-start(f32[256,32,128]{2,0,1:T(8,128)} %get-tuple-element.18) | copy-start | bytes 12582916
  280.7 7.8 %copy-start.6 = (f32[256,32,128]{2,0,1:T(8,128)S(1)}, f32[256,32,128]{2,0,1:T(8,128)}, u32[]{:S(2)}) copy-start(f32[256,32,128]{2,0,1:T(8,128)} %get-tuple-element.20) | copy-start | bytes 12582916
  280.7 7.8 %copy-start.14 = (f32[256,32,128]{2,1,0:T(8,128)S(1)}, f32[256,32,128]{2,1,0:T(8,128)}, u32[]{:S(2)}) copy-start(f32[256,32,128]{2,1,0:T(8,128)} %fusion.46) | copy-start | bytes 12582916
  297.0 3.0 copy-start.27
  305.1 23.6 %all-to-all-start.4 = ((bf16[256,8,256]{2,0,1:T(8,128)(2,1)}), bf16[256,8,256]{2,0,1:T(8,128)(2,1)S(1)}, u32[]{:S(2)}, u32[]{:S(2)}) async-start(bf16[256,8,256]{2,0,1:T(8,128)(2,1)} %get-tuple-element.28), calls=%async_computation.4 | async-start | bytes 2097152 | tf_op jit(solution)/shard_map/all_to_all | solution.py:122
  309.3 9.8 %copy-start.10 = (f32[256,32,128]{2,0,1:T(8,128)S(1)}, f32[256,32,128]{2,0,1:T(8,128)}, u32[]{:S(2)}) copy-start(f32[256,32,128]{2,0,1:T(8,128)} %get-tuple-element.6) | copy-start | bytes 12582916
  319.1 4.1 %copy-start.5 = (f32[256,32,128]{2,0,1:T(8,128)S(1)}, f32[256,32,128]{2,0,1:T(8,128)}, u32[]{:S(2)}) copy-start(f32[256,32,128]{2,0,1:T(8,128)} %get-tuple-element.5) | copy-start | bytes 12582916
  328.7 20.0 %all-to-all-start.7 = ((bf16[256,8,256]{2,0,1:T(8,128)(2,1)}), bf16[256,8,256]{2,0,1:T(8,128)(2,1)}, u32[]{:S(2)}, u32[]{:S(2)}) async-start(bf16[256,8,256]{2,0,1:T(8,128)(2,1)} %get-tuple-element.27), calls=%async_computation.7 | async-start | bytes 2097152 | tf_op jit(solution)/shard_map/all_to_all | solution.py:123
  333.2 5.1 %copy-start.3 = (f32[256,32,128]{2,1,0:T(8,128)S(1)}, f32[256,32,128]{2,1,0:T(8,128)}, u32[]{:S(2)}) copy-start(f32[256,32,128]{2,1,0:T(8,128)} %fusion.109) | copy-start | bytes 12582916
  333.2 5.9 %copy-start.4 = (f32[256,32,128]{2,1,0:T(8,128)S(1)}, f32[256,32,128]{2,1,0:T(8,128)}, u32[]{:S(2)}) copy-start(f32[256,32,128]{2,1,0:T(8,128)} %fusion.106) | copy-start | bytes 12582916
  345.0 9.4 %copy-start.18 = (bf16[256,2048]{1,0:T(8,128)(2,1)S(1)}, bf16[256,2048]{1,0:T(8,128)(2,1)}, u32[]{:S(2)}) copy-start(bf16[256,2048]{1,0:T(8,128)(2,1)} %copy-done.17) | copy-start | bytes 3145732
  345.0 9.4 %copy-start.20 = (bf16[256,2048]{1,0:T(8,128)(2,1)S(1)}, bf16[256,2048]{1,0:T(8,128)(2,1)}, u32[]{:S(2)}) copy-start(bf16[256,2048]{1,0:T(8,128)(2,1)} %copy-done.19) | copy-start | bytes 3145732
  354.4 3.7 %copy-start.16 = (bf16[64,4,2048]{2,0,1:T(8,128)(2,1)S(1)}, bf16[64,4,2048]{2,0,1:T(8,128)(2,1)}, u32[]{:S(2)}) copy-start(bf16[64,4,2048]{2,0,1:T(8,128)(2,1)} %copy-done.15) | copy-start | bytes 3145732
  354.4 3.7 %copy-start.22 = (bf16[256,2048]{1,0:T(8,128)(2,1)S(1)}, bf16[256,2048]{1,0:T(8,128)(2,1)}, u32[]{:S(2)}) copy-start(bf16[256,2048]{1,0:T(8,128)(2,1)} %copy-done.21) | copy-start | bytes 3145732
  354.4 3.7 %copy-start.23 = (f32[2048,256]{0,1:T(8,128)S(1)}, f32[2048,256]{0,1:T(8,128)}, u32[]{:S(2)}) copy-start(f32[2048,256]{0,1:T(8,128)} %copy.148) | copy-start | bytes 6291460
  354.4 5.6 %copy-start.1 = (s32[8,512]{1,0:T(8,128)S(1)}, s32[8,512]{1,0:T(8,128)}, u32[]{:S(2)}) copy-start(s32[8,512]{1,0:T(8,128)} %param.10) | copy-start | bytes 49156
where the time goes:
time: 365 us; the launch traced here: 360 us
  matrix products  190 us (52%)
  blocking collectives  62.1 us (17%)
  local copies, waits for them, and re-layouts  42.9 us (12%)
  starting transfers between devices  26.2 us (7%)
  waiting for transfers between devices  21.6 us (6%)
  other arithmetic  16.6 us (5%)
    dot_general x3, matrix products, forward_dft(): jnp.einsum('cks,sj->ckj', twist_re, sin_cols, precision=PRECISE)  33 us
    all_to_all x1, blocking collectives, per_device(): lax.all_to_all(grad_out, 'tp', split_axis=1, concat_axis=0, tiled=True)  31.8 us
    all_to_all x1, blocking collectives, per_device(): lax.all_to_all(key_rows, 'ctx', split_axis=0, concat_axis=0, tiled=True)  30.2 us
    dot_general x3, matrix products, inverse_dft(): jnp.einsum('ckj,js->cks', spec_re, sin_cols, precision=PRECISE)  21.6 us
    dot_general x3, matrix products, inverse_dft(): jnp.einsum('ckj,js->cks', spec_im, cos_cols, precision=PRECISE)  18.9 us
    dot_general x3, matrix products, forward_dft(): jnp.einsum('cks,sj->ckj', twist_im, cos_cols, precision=PRECISE)  18.5 us
    all_to_all x1, waiting for transfers between devices, per_device(): lax.all_to_all(value_rows, 'ctx', split_axis=0, concat_axis=0, tiled=True)  17.6 us
    dot_general x3, matrix products, forward_dft(): jnp.einsum('cks,sj->ckj', twist_re, cos_cols, precision=PRECISE)  17 us
  transfers between devices with their start and end apart: 6, of which 3 were waited for; matrix products, arithmetic and copies ran while one was open for 28% of the time, Pallas kernels for 0%

commit v1 on v0

v1 whole, which is shorter than its diff:
```python
import functools
import math

import jax
import jax.numpy as jnp
import ml_dtypes
import numpy as np
from jax import lax
from jax.experimental import pallas as pl
from jax.experimental.pallas import tpu as pltpu
from jax.sharding import PartitionSpec as P

F32 = jnp.float32
BF16 = jnp.bfloat16
ROWS = 16
VMEM_LIMIT = 63_000_000


@functools.lru_cache(maxsize=None)
def dense_tables(shards, span):
    points = 2 * shards * span
    half = span // 2
    r = np.arange(span)
    forward = np.zeros((shards, 2 * span, 2 * span))
    for k1 in range(1, shards):
        bins = k1 + 2 * shards * np.arange(span)
        angle = (bins[:, None] * r[None, :] % points) * (2.0 * np.pi / points)
        cos, sin = np.cos(angle), np.sin(angle)
        forward[k1] = np.block([[cos, sin], [-sin, cos]])
    for place, k1 in ((0, 0), (1, shards)):
        bins = k1 + 2 * shards * np.arange(half)
        angle = (bins[:, None] * r[None, :] % points) * (2.0 * np.pi / points)
        columns = slice(place * span, place * span + span)
        forward[0, place * half : place * half + half, columns] = np.cos(angle)
        forward[0, span + place * half : span + place * half + half, columns] = -np.sin(angle)
    forward[0, span, :span] = 1.0 - 2.0 * (r % 2)
    inverse = 2.0 * np.transpose(forward, (0, 2, 1))
    inverse[0, :, 0] *= 0.5
    inverse[0, :, span] *= 0.5

    def parts(table):
        table = table.astype(np.float32)
        high = table.astype(ml_dtypes.bfloat16)
        low = (table - high.astype(np.float32)).astype(ml_dtypes.bfloat16)
        return high, low

    return parts(forward), parts(inverse)


def plus(a, b):
    if a is None:
        return b
    return a if b is None else a + b


def minus(a, b):
    if b is None:
        return a
    return -b if a is None else a - b


def turned(z, step, count, sign):
    angle = sign * 2.0 * math.pi * (step % count) / count
    cos, sin = math.cos(angle), math.sin(angle)
    re, im = z
    if abs(sin) < 1e-9:
        return z if cos > 0 else (minus(None, re), minus(None, im))
    if abs(cos) < 1e-9:
        return (minus(None, im), re) if sin > 0 else (im, minus(None, re))
    if re is None and im is None:
        return z
    if im is None:
        return (re * cos, re * sin)
    if re is None:
        return (im * -sin, im * cos)
    if abs(abs(cos) - abs(sin)) < 1e-9:
        root = math.sqrt(0.5)
        first = re - im if sin * cos > 0 else re + im
        second = re + im if sin * cos > 0 else im - re
        c = root if cos > 0 else -root
        return (first * c, second * c)
    return (re * cos - im * sin, im * cos + re * sin)


def spread(values, sign):
    count = len(values)
    if count == 1:
        return values
    half = count // 2
    low, high = values[:half], values[half:]
    even = [(plus(a[0], b[0]), plus(a[1], b[1])) for a, b in zip(low, high)]
    odd = [
        turned((minus(a[0], b[0]), minus(a[1], b[1])), step, count, sign)
        for step, (a, b) in enumerate(zip(low, high))
    ]
    out = [None] * count
    out[0::2] = spread(even, sign)
    out[1::2] = spread(odd, sign)
    return out


def gather_up(values, sign):
    count = len(values)
    if count == 1:
        return values
    half = count // 2
    even = gather_up(values[0::2], sign)
    odd = [turned(z, step, count, sign) for step, z in enumerate(gather_up(values[1::2], sign))]
    return [(plus(a[0], b[0]), plus(a[1], b[1])) for a, b in zip(even, odd)] + [
        (minus(a[0], b[0]), minus(a[1], b[1])) for a, b in zip(even, odd)
    ]


def dot(a, b):
    return jnp.dot(a, b, preferred_element_type=F32)


def shard_transform(load, high_ref, low_ref=None):
    shards, rows, width = high_ref.shape
    span = rows // 2
    lanes = min(128, width)

    def body(step, carry):
        first = pl.multiple_of(step * ROWS, ROWS)
        for lane in range(0, width, lanes):
            values = [(load(i, pl.ds(first, ROWS), pl.ds(lane, lanes)), None) for i in range(shards)]
            values = spread(values + [(None, None)] * shards, -1)
            for k1 in range(shards):
                pair = (values[0][0], values[shards][0]) if k1 == 0 else values[k1]
                for part, value in enumerate(pair):
                    where = pl.ds(pl.multiple_of(part * span + first, ROWS), ROWS)
                    high = value.astype(BF16)
                    high_ref[k1, where, pl.ds(lane, lanes)] = high
                    if low_ref is not None:
                        low = (value - high.astype(F32)).astype(BF16)
                        low_ref[k1, where, pl.ds(lane, lanes)] = low
        return carry

    lax.fori_loop(0, span // ROWS, body, 0)


def shard_inverse(slab_ref, store):
    shards, rows, width = slab_ref.shape
    span = rows // 2
    lanes = min(128, width)

    def body(step, carry):
        first = pl.multiple_of(step * ROWS, ROWS)
        for lane in range(0, width, lanes):
            def load(k1, part):
                where = pl.ds(pl.multiple_of(part * span + first, ROWS), ROWS)
                return slab_ref[k1, where, pl.ds(lane, lanes)]

            values = [(load(0, 0), None)]
            values += [(load(k1, 0), load(k1, 1)) for k1 in range(1, shards)]
            values += [(load(0, 1), None)] + [(None, None)] * (shards - 1)
            values = gather_up(values, 1)
            for i in range(shards):
                store(i, pl.ds(first, ROWS), pl.ds(lane, lanes), values[i][0])
        return carry

    lax.fori_loop(0, span // ROWS, body, 0)


def bin_product(a, b, conjugate, first_slab):
    span = a.shape[0] // 2
    ar, ai, br, bi = a[:span], a[span:], b[:span], b[span:]
    cross = ai * bi
    shared = cross
    im = ai * br - ar * bi if conjugate else ar * bi + ai * br
    if first_slab is not False:
        alone = (lax.broadcasted_iota(jnp.int32, (span, 1), 0) == 0) & first_slab
        shared = jnp.where(alone, 0.0, cross)
        im = jnp.where(alone, cross, im)
    re = ar * br + shared if conjugate else ar * br - shared
    return jnp.concatenate([re.astype(BF16), im.astype(BF16)], axis=0)


def filter_kernel(filters_ref, fh_ref, fl_ref, after_ref, spec_ref, seq_ref, high_ref, low_ref):
    slab = pl.program_id(0)
    shards, span = seq_ref.shape[:2]

    @pl.when(slab == 0)
    def _():
        for i in range(shards):
            seq_ref[i] = filters_ref[:, i * span : (i + 1) * span].T
        shard_transform(lambda i, r, c: seq_ref[i, r, c], high_ref, low_ref)

    high = high_ref[slab]
    spec_ref[0] = dot(fh_ref[0], high) + dot(fh_ref[0], low_ref[slab]) + dot(fl_ref[0], high)


def conv_kernel(conjugate, scale, n_in, turn_ref, *refs):
    pieces, refs = refs[:n_in], refs[n_in:]
    bias_ref, other_hbm, fh_hbm, ih_hbm, after_ref, out_ref, spec_hbm = refs[:7]
    fh_ref, ih_ref, other_ref, spec_ref, high_ref, slab_ref, in_sems, out_sems = refs[7:15]
    seq_ref = pieces[0] if n_in == 1 else refs[15]
    shards = fh_ref.shape[0]

    def fetch(which, slab):
        source, target = ((fh_hbm, fh_ref), (other_hbm, other_ref), (ih_hbm, ih_ref))[which]
        return pltpu.make_async_copy(source.at[slab], target.at[slab], in_sems.at[which, slab])

    def keep(slab):
        return pltpu.make_async_copy(spec_ref.at[slab], spec_hbm.at[slab], out_sems.at[slab])

    for slab in range(shards):
        for which in range(3):
            fetch(which, slab).start()
    if n_in > 1:
        for number in range(n_in):
            seq_ref[turn_ref[0] ^ number] = pieces[number][...]

    def load(i, rows, lanes):
        return seq_ref[i, rows, lanes].astype(F32)

    shard_transform(load, high_ref)

    def forward(slab):
        fetch(0, slab).wait()
        spec_ref[slab] = dot(fh_ref[slab], high_ref[slab])
        keep(slab).start()

    forward(0)
    for slab in range(shards):
        if slab + 1 < shards:
            forward(slab + 1)
        fetch(1, slab).wait()
        product = bin_product(spec_ref[slab], other_ref[slab], conjugate, slab == 0)
        fetch(2, slab).wait()
        slab_ref[slab] = dot(ih_ref[slab], product)

    def store(i, rows, lanes, value):
        direct = bias_ref[:, lanes] * load(i, rows, lanes)
        out_ref[i, rows, lanes] = (direct + scale * value).astype(BF16)

    shard_inverse(slab_ref, store)
    for slab in range(shards):
        keep(slab).wait()


def correlation_kernel(scale, spec_ref, other_ref, ih_ref, out_ref, slab_ref, seq_ref):
    slab = pl.program_id(0)
    shards = pl.num_programs(0)
    span = seq_ref.shape[1]
    slab_ref[slab] = dot(ih_ref[0], bin_product(spec_ref[0], other_ref[0], True, slab == 0))

    @pl.when(slab == shards - 1)
    def _():
        def store(i, rows, lanes, value):
            seq_ref[i, rows, lanes] = scale * value

        shard_inverse(slab_ref, store)
        for i in range(seq_ref.shape[0]):
            out_ref[:, i * span : (i + 1) * span] = seq_ref[i].T


def placement(own_ref, select_ref):
    tokens, slots = select_ref.shape
    token = lax.broadcasted_iota(jnp.int32, (tokens, slots), 0)
    select_ref[...] = jnp.where(token == own_ref[...], 1.0, 0.0).astype(BF16)


def pack_kernel(shards, turn_ref, *refs):
    sources, outs = refs[: -shards - 3], refs[-shards - 3 : -3]
    held, in_sems, out_sems = refs[-3:]
    rows = sources[0].shape[0] // shards

    def read(number, place):
        start = pl.multiple_of((turn_ref[0] ^ number) * rows, rows)
        return pltpu.make_async_copy(
            sources[place].at[pl.ds(start, rows)],
            held.at[number, pl.ds(place * rows, rows)],
            in_sems.at[number, place],
        )

    def write(number):
        return pltpu.make_async_copy(held.at[number], outs[number], out_sems.at[number])

    for number in range(shards):
        for place in range(len(sources)):
            read(number, place).start()
    for number in range(shards):
        for place in range(len(sources)):
            read(number, place).wait()
        write(number).start()
    for number in range(shards):
        write(number).wait()


def by_owner(turn, outs, value_ref):
    width = outs[0].shape[-1]
    parts = value_ref.shape[1] // width
    if len(outs) == 1:
        for part in range(parts):
            outs[0][part] = value_ref[:, part * width : (part + 1) * width]
        return
    for step in range(len(outs) // parts):

        @pl.when(pl.program_id(0) == step)
        def _(step=step):
            for part in range(parts):
                lanes = pl.ds(pl.multiple_of(((turn % parts) ^ part) * width, width), width)
                outs[step * parts + part][...] = value_ref[:, lanes]


def gate_kernel(*refs):
    pass


def settle_signal_kernel(shards, turn_ref, own_ref, after_ref, *refs):
    slots, (key_out, value_out), outs = refs[:shards], refs[shards : shards + 2], refs[shards + 2 : -2]
    select_ref, product_ref = refs[-2:]

    @pl.when(pl.program_id(0) == 0)
    def _():
        placement(own_ref, select_ref)

    slot_rows = slots[0].shape[0] // 2
    key = dot(select_ref[...], jnp.concatenate([slot[:slot_rows] for slot in slots], axis=0))
    value = dot(select_ref[...], jnp.concatenate([slot[slot_rows:] for slot in slots], axis=0))
    key_out[...] = key.astype(BF16)
    value_out[...] = value.astype(BF16)
    product_ref[...] = (key * value).astype(BF16)
    by_owner(turn_ref[0], outs, product_ref)


def settle_query_kernel(tensor, source_ref, own_ref, rows_ref, *refs):
    pieces = refs[:tensor]
    grad_out, query_out, out_ref, select_ref, product_ref = refs[-5:]

    @pl.when(pl.program_id(0) == 0)
    def _():
        placement(own_ref, select_ref)

    rows = pieces[0].shape[0]
    for number, piece in enumerate(pieces):
        start = pl.multiple_of(source_ref[number] * rows, rows)
        grad_out[pl.ds(start, rows), :] = piece[...]
    query = dot(select_ref[...], rows_ref[...])
    query_out[...] = query.astype(BF16)
    product_ref[...] = (query * grad_out[...].astype(F32)).astype(BF16)
    by_owner(None, [out_ref], product_ref)


def final_kernel(shared_ref, a_ref, b_ref, after_ref, a_out, b_out):
    width = shared_ref.shape[2]
    for part in range(shared_ref.shape[0]):
        lanes = slice(part * width, (part + 1) * width)
        shared = shared_ref[part].astype(F32)
        a_out[:, lanes] = (a_ref[:, lanes].astype(F32) * shared).astype(BF16)
        b_out[:, lanes] = (b_ref[:, lanes].astype(F32) * shared).astype(BF16)


def cost(flops, moved):
    return pl.CostEstimate(flops=int(flops), bytes_accessed=int(moved), transcendentals=0)


def params():
    return pltpu.CompilerParams(
        dimension_semantics=("arbitrary",), vmem_limit_bytes=VMEM_LIMIT
    )


def whole(shape):
    return pl.BlockSpec(shape, lambda j, *turn: (0,) * len(shape))


def slab_of(shape):
    return pl.BlockSpec((1,) + shape[1:], lambda j, *turn: (j, 0, 0))


UNREAD = pl.BlockSpec(memory_space=pl.ANY)


def shape_of(shape, dtype):
    return jax.ShapeDtypeStruct(shape, dtype)


def filter_spectrum(filters, tables, after):
    (fh, fl), _ = tables
    width, length = filters.shape
    shards, rows, _ = fh.shape
    spec = (shards, rows, width)
    return pl.pallas_call(
        filter_kernel,
        grid=(shards,),
        in_specs=[whole(filters.shape), slab_of(fh.shape), slab_of(fl.shape), UNREAD],
        out_specs=slab_of(spec),
        out_shape=shape_of(spec, F32),
        scratch_shapes=[
            pltpu.VMEM((shards, rows // 2, width), F32),
            pltpu.VMEM(spec, BF16),
            pltpu.VMEM(spec, BF16),
        ],
        compiler_params=params(),
        cost_estimate=cost(6 * shards * rows * rows * width, 4 * filters.size + 8 * fh.size),
        name="filter_spectrum",
    )(filters, fh, fl, after)


def convolve(turn, pieces, bias, other, tables, conjugate, after):
    (fh, _), (ih, _) = tables
    shards, rows, _ = fh.shape
    tokens, width = pieces[0].shape[-2:]
    spec = (shards, rows, width)
    seq = (shards, tokens, width)
    length = shards * tokens
    scale = 1.0 / (2 * length * math.sqrt(length))
    return pl.pallas_call(
        functools.partial(conv_kernel, conjugate, scale, len(pieces)),
        grid_spec=pltpu.PrefetchScalarGridSpec(
            num_scalar_prefetch=1,
            grid=(1,),
            in_specs=[whole(piece.shape) for piece in pieces] + [whole(bias.shape)] + [UNREAD] * 4,
            out_specs=[whole(seq), UNREAD],
            scratch_shapes=[
                pltpu.VMEM(fh.shape, BF16),
                pltpu.VMEM(ih.shape, BF16),
                pltpu.VMEM(spec, F32),
                pltpu.VMEM(spec, F32),
                pltpu.VMEM(spec, BF16),
                pltpu.VMEM(spec, F32),
                pltpu.SemaphoreType.DMA((3, shards)),
                pltpu.SemaphoreType.DMA((shards,)),
            ]
            + [pltpu.VMEM(seq, BF16)] * (len(pieces) > 1),
        ),
        out_shape=[shape_of(seq, BF16), shape_of(spec, F32)],
        compiler_params=params(),
        cost_estimate=cost(4 * shards * rows * rows * width, 4 * fh.size + 12 * shards * rows * width),
        name="convolve_backward" if conjugate else "convolve_forward",
    )(turn, *pieces, bias, other, fh, ih, after)


def correlate(spec_a, spec_b, tables):
    _, (ih, _) = tables
    shards, rows, width = spec_a.shape
    length = shards * rows // 2
    scale = 1.0 / (2 * length * math.sqrt(length))
    return pl.pallas_call(
        functools.partial(correlation_kernel, scale),
        grid=(shards,),
        in_specs=[slab_of(spec_a.shape), slab_of(spec_b.shape), slab_of(ih.shape)],
        out_specs=whole((width, length)),
        out_shape=shape_of((width, length), F32),
        scratch_shapes=[
            pltpu.VMEM(spec_a.shape, F32),
            pltpu.VMEM((shards, rows // 2, width), F32),
        ],
        compiler_params=params(),
        cost_estimate=cost(4 * shards * rows * rows * width, 2 * ih.size + 12 * spec_a.size),
        name="filter_gradient",
    )(spec_a, spec_b, ih)


def pack(turn, arrays, shards):
    rows, channels = arrays[0].shape
    rows = len(arrays) * rows // shards
    moved = 4 * len(arrays) * arrays[0].size
    return pl.pallas_call(
        functools.partial(pack_kernel, shards),
        grid_spec=pltpu.PrefetchScalarGridSpec(
            num_scalar_prefetch=1,
            grid=(1,),
            in_specs=[pl.BlockSpec(memory_space=pl.ANY)] * len(arrays),
            out_specs=[pl.BlockSpec(memory_space=pl.ANY)] * shards,
            scratch_shapes=[
                pltpu.VMEM((shards, rows, channels), arrays[0].dtype),
                pltpu.SemaphoreType.DMA((shards, len(arrays))),
                pltpu.SemaphoreType.DMA((shards,)),
            ],
        ),
        out_shape=[shape_of((rows, channels), arrays[0].dtype)] * shards,
        compiler_params=params(),
        cost_estimate=cost(0, moved),
        name="pack_rows",
    )(turn, *arrays)


def column_plan(channels, shards, lanes):
    width = channels // shards
    parts = min(shards, max(1, lanes // width))
    return width, parts, parts * width, shards // parts


def column(rows, block):
    return pl.BlockSpec((rows, block), lambda j: (0, j))


def turned_column(rows, block, parts, pieces):
    if pieces:
        return pl.BlockSpec((rows, block), lambda j, turn: (0, j ^ (turn[0] // parts)))
    return pl.BlockSpec((rows, block), lambda j, turn: (0, j))


def gate(value, after):
    return pl.pallas_call(
        gate_kernel,
        in_specs=[UNREAD] * (1 + len(after)),
        out_specs=UNREAD,
        out_shape=shape_of(value.shape, value.dtype),
        input_output_aliases={0: 0},
        name="gate",
    )(value, *after)


def settle_signal(turn, own, slots, tokens, n_out, after):
    shards = len(slots)
    slot_rows, channels = slots[0].shape
    count = shards * slot_rows // 2
    width, parts, block, steps = column_plan(channels, shards, 512)
    seq = shape_of((tokens, channels), BF16)
    column_at = functools.partial(turned_column, block=block, parts=parts, pieces=n_out > 1)
    if n_out > 1:
        out_spec, out_shape = whole((tokens, width)), shape_of((tokens, width), BF16)
    else:
        out_spec = pl.BlockSpec((parts, tokens, width), lambda j, turn: (j, 0, 0))
        out_shape = shape_of((shards, tokens, width), BF16)
    outs = pl.pallas_call(
        functools.partial(settle_signal_kernel, shards),
        grid_spec=pltpu.PrefetchScalarGridSpec(
            num_scalar_prefetch=1,
            grid=(steps,),
            in_specs=[whole(own.shape), UNREAD] + [column_at(slot_rows)] * shards,
            out_specs=[column_at(tokens)] * 2 + [out_spec] * n_out,
            scratch_shapes=[pltpu.VMEM((tokens, count), BF16), pltpu.VMEM((tokens, block), BF16)],
        ),
        out_shape=[seq, seq] + [out_shape] * n_out,
        compiler_params=params(),
        cost_estimate=cost(4 * tokens * count * channels, 4 * count * channels + 6 * tokens * channels),
        name="settle_signal",
    )(turn, own, after, *slots)
    return outs[0], outs[1], outs[2:]


def settle_query(own, rows, sources, pieces, tokens, shards, after):
    count, channels = rows.shape
    width, parts, block, steps = column_plan(channels, shards, 512)
    seq = shape_of((tokens, channels), BF16)
    return pl.pallas_call(
        functools.partial(settle_query_kernel, len(pieces)),
        grid=(steps,),
        in_specs=[pl.BlockSpec(memory_space=pltpu.SMEM), whole(own.shape), column(count, block)]
        + [column(piece.shape[0], block) for piece in pieces]
        + [UNREAD] * len(after),
        out_specs=[column(tokens, block)] * 2
        + [pl.BlockSpec((parts, tokens, width), lambda j: (j, 0, 0))],
        out_shape=[seq, seq, shape_of((shards, tokens, width), BF16)],
        scratch_shapes=[pltpu.VMEM((tokens, count), BF16), pltpu.VMEM((tokens, block), BF16)],
        compiler_params=params(),
        cost_estimate=cost(2 * tokens * count * channels, 2 * count * channels + 8 * tokens * channels),
        name="settle_query",
    )(sources, own, rows, *pieces, *after)


def final_products(shared, a, b, after, name):
    shards, tokens, width = shared.shape
    _, parts, block, steps = column_plan(a.shape[1], shards, 1024)
    return pl.pallas_call(
        final_kernel,
        grid=(steps,),
        in_specs=[
            pl.BlockSpec((parts, tokens, width), lambda j: (j, 0, 0)),
            column(tokens, block), column(tokens, block), UNREAD,
        ],
        out_specs=[column(tokens, block)] * 2,
        out_shape=[shape_of(a.shape, BF16)] * 2,
        compiler_params=params(),
        cost_estimate=cost(2 * a.size, 10 * a.size),
        name=name,
    )(shared, a, b, after)


def permuted(pieces):
    shards = len(pieces)
    order = sorted(range(1, shards), key=lambda number: (number < 2, number & 1, number))
    received = {
        number: lax.ppermute(pieces[number], "ctx", [(i, i ^ number) for i in range(shards)])
        for number in order
    }
    return [pieces[0]] + [received[number] for number in range(1, shards)]


def exchange(value):
    return lax.all_to_all(value, "ctx", split_axis=0, concat_axis=0, tiled=True)


def per_device(query_rows, key_rows, value_rows, positions, filters, bias_term, grad_out):
    shards = lax.axis_size("ctx")
    ctx_index = lax.axis_index("ctx")
    slots, channels = query_rows.shape
    slot_rows = slots // shards
    tokens = filters.shape[1] // shards
    tables = dense_tables(shards, tokens)

    tensor = lax.axis_size("tp")
    tensor_index = lax.axis_index("tp")
    turn = ctx_index.astype(jnp.int32).reshape(1)
    bias = bias_term.reshape(1, -1)

    query_recv = exchange(query_rows)

    pieces = []
    for shift in range(tensor):
        target = (tensor_index + shift) % tensor
        piece = lax.dynamic_slice_in_dim(grad_out, target * channels, channels, 1)
        if shift:
            piece = lax.ppermute(piece, "tp", [(i, (i + shift) % tensor) for i in range(tensor)])
        pieces.append(piece)
    grad_sources = (tensor_index - jnp.arange(tensor, dtype=jnp.int32)) % tensor

    both_packed = pack(turn, [key_rows, value_rows], shards)
    both_slots = permuted(both_packed)
    own = lax.dynamic_slice_in_dim(positions, ctx_index * slot_rows, slot_rows, 1)
    own_turned = jnp.concatenate(
        [lax.dynamic_slice_in_dim(own, ctx_index ^ number, 1, 0) for number in range(shards)], axis=1
    )

    filter_spec = filter_spectrum(filters, tables, both_packed[0])
    grad_seq, query_seq, grad_conv = settle_query(
        own.reshape(1, slots), query_recv, grad_sources, pieces, tokens, shards, [filter_spec]
    )
    grad_conv = gate(grad_conv, both_slots[1:])
    grad_recv = exchange(grad_conv)
    key_seq, value_seq, signal = settle_signal(
        turn, own_turned, both_slots, tokens, 1, grad_conv
    )
    signal_recv = [exchange(signal[0])]
    grad_signal, grad_spec = convolve(
        turn, [grad_recv], bias, filter_spec, tables, True, signal[0]
    )
    grad_signal_recv = exchange(grad_signal)
    conv_out, signal_spec = convolve(
        turn, signal_recv, bias, filter_spec, tables, False, grad_signal
    )
    conv_recv = exchange(conv_out)
    grad_filters = correlate(grad_spec, signal_spec, tables)
    grad_key, grad_value = final_products(
        grad_signal_recv, value_seq, key_seq, grad_filters, "key_value_gradients"
    )
    output, grad_query = final_products(
        conv_recv, query_seq, grad_seq, grad_key, "output_and_query_gradient"
    )
    return output, grad_query, grad_key, grad_value, grad_filters


def solution(mesh):
    return jax.shard_map(
        per_device,
        mesh=mesh,
        in_specs=(
            P("ctx", "tp"),
            P("ctx", "tp"),
            P("ctx", "tp"),
            P(),
            P(("tp", "ctx"), None),
            P(("tp", "ctx")),
            P(("ctx", "tp"), None),
        ),
        out_specs=(
            P("ctx", "tp"),
            P("ctx", "tp"),
            P("ctx", "tp"),
            P("ctx", "tp"),
            P(("tp", "ctx"), None),
        ),
        check_vma=False,
    )
```

time: 365 us -> 158 us (0.43)
  matrix products: 190 us -> 0 us
  Pallas kernels: 0 us -> 68.1 us
  blocking collectives: 62.1 us -> 0 us
  local copies, waits for them, and re-layouts: 42.9 us -> 5.97 us
  waiting for transfers between devices: 21.6 us -> 50.9 us
  other arithmetic: 16.6 us -> 0.49 us
  starting transfers between devices: 26.2 us -> 30.4 us
    dot_general x36 -> x0, matrix products: 190 us -> none  [the longest x3 33 us: forward_dft(): jnp.einsum('cks,sj->ckj', twist_re, sin_cols, precision=PRECISE)]
    pallas_call x0 -> x10, Pallas kernels: none -> 68.1 us  [the longest x2 25.7 us: convolve(): pl.pallas_call(functools.partial(conv_kernel, conjugate, scale, len(piece...]
    all_to_all x2 -> x0, blocking collectives: 62.1 us -> none  [the longest x1 31.8 us: per_device(): lax.all_to_all(grad_out, 'tp', split_axis=1, concat_axis=0, tiled=True)]
    ppermute x0 -> x10, waiting for transfers between devices: none -> 35.3 us  [the longest x3 20.4 us: per_device(): lax.ppermute(piece, 'tp', [(i, (i + shift) % tensor) for i in range(tenso...]
    convert_element_type x6 -> x0, other arithmetic: 15 us -> none  [the longest x1 5.08 us: per_device(): (bias_term[:, None] * grad_wide + factor * backward_conv).astype(jnp.bflo...]
    scatter x3 -> x0, local copies, waits for them, and re-layouts: 14.9 us -> none  [settle_rows(): return empty.at[target].set(rows, mode='drop')]
    ppermute x0 -> x10, starting transfers between devices: none -> 10.8 us  [the longest x7 6.19 us: permuted(): lax.ppermute(pieces[number], 'ctx', [(i, i ^ number) for i in range(shard...]
    all_to_all x5 -> x0, local copies, waits for them, and re-layouts: 9.08 us -> none  [the longest x2 3.82 us: per_device(): lax.all_to_all(grad_conv.T, 'ctx', split_axis=0, concat_axis=1, tiled=True)]
  transfers between devices with their start and end apart: 6 -> 15, of which waited for: 3 -> 10; matrix products, arithmetic and copies ran while one was open for 28% -> 3% of each run, Pallas kernels for 0% -> 42%
where the time goes in v1:
time: 158 us; the launch traced here: 157 us
  Pallas kernels  68.1 us (43%)
  waiting for transfers between devices  50.9 us (32%)
  starting transfers between devices  30.4 us (19%)
  local copies, waits for them, and re-layouts  5.97 us (4%)
    pallas_call x2, Pallas kernels, convolve(): pl.pallas_call(functools.partial(conv_kernel, conjugate, scale, len(piece...  25.7 us
    ppermute x3, waiting for transfers between devices, per_device(): lax.ppermute(piece, 'tp', [(i, (i + shift) % tensor) for i in range(tenso...  20.4 us
    all_to_all x5, starting transfers between devices, exchange(): return lax.all_to_all(value, 'ctx', split_axis=0, concat_axis=0, tiled=True)  19.6 us
    all_to_all x5, waiting for transfers between devices, exchange(): return lax.all_to_all(value, 'ctx', split_axis=0, concat_axis=0, tiled=True)  15.7 us
    ppermute x7, waiting for transfers between devices, permuted(): lax.ppermute(pieces[number], 'ctx', [(i, i ^ number) for i in range(shard...  14.9 us
    pallas_call x1, Pallas kernels, filter_spectrum(): pl.pallas_call(filter_kernel, grid=(shards,), in_specs=[whole(filters.sha...  12.2 us
    pallas_call x1, Pallas kernels, correlate(): pl.pallas_call(functools.partial(correlation_kernel, scale), grid=(shards...  10.6 us
    ppermute x7, starting transfers between devices, permuted(): lax.ppermute(pieces[number], 'ctx', [(i, i ^ number) for i in range(shard...  6.19 us
  transfers between devices with their start and end apart: 15, of which 10 were waited for; matrix products, arithmetic and copies ran while one was open for 3% of the time, Pallas kernels for 42%

profile of v1, /device:TPU:0, one launch (start us, length us, event | category | flops | bytes accessed | tf_op | source)
XLA Modules:
  0.0 156.7 jit_solution(14069463678309035272)
XLA Ops:
  0.6 5.2 %all-to-all-start = ((bf16[8,64,2048]{2,1,0:T(8,128)(2,1)}), bf16[8,64,2048]{2,1,0:T(8,128)(2,1)S(1)}, u32[]{:S(2)}, u32[]{:S(2)}) async-start(bf16[8,64,2048]{2,1,0:T(8,128)(2,1)} %bitcast.5), calls=%async_computation | async-start | bytes 4194304 | tf_op jit(solution)/shard_map/all_to_all | solution.py:586
  5.8 3.7 %pack_rows.1 = (bf16[128,2048]{1,0:T(8,128)(2,1)}, bf16[128,2048]{1,0:T(8,128)(2,1)}, bf16[128,2048]{1,0:T(8,128)(2,1)}, bf16[128,2048]{1,0:T(8,128)(2,1)}, bf16...) custom-call(s32[1]{0:T(128)} %bitcast.turn_ref, ...), custom_call_target="tpu_custom_call" | custom-call | bytes 8388608 | tf_op jit(solution)/shard_map/pack_rows/pallas_call | solution.py:461
  9.5 0.6 collective-permute-start.3
  10.1 1.7 %collective-permute-start.4 = (bf16[128,2048]{1,0:T(8,128)(2,1)}, bf16[128,2048]{1,0:T(8,128)(2,1)S(1)}, u32[]{:S(2)}, u32[]{:S(2)}) collective-permute-start(bf16[128,2048]{1,0:T(8,128)(2,1)} %get-tuple-element.30), channel_id=1, source_target_pairs={{0,8},{4,12},{8,0},{12,4},{16,24},{20,28},{24,16},{28,20},{1,9},{5... | collective-permute-start | bytes 1572872 | tf_op jit(solution)/shard_map/ppermute | solution.py:579
  11.7 2.2 %constant_dynamic-slice_fusion = (bf16[64,2048]{1,0:T(8,128)(2,1)}, bf16[64,2048]{1,0:T(8,128)(2,1)}, bf16[64,2048]{1,0:T(8,128)(2,1)}, bf16[64,2048]{1,0:T(8,128)(2,1)}) fusion(bf16[64,8192]{1,0:T(8,128)(2,1)} %param.16, s32[]{:T(128)S(6)} %select_n.108, s32[]{:T(128)S(6)} %select_n.104, s32[]{:T(128)S(6)} %select_n.102, s32[]{:T(128)S(6)} %select_n.106), kind=kLoop, calls=%fused_computation.3 | loop fusion | bytes 2097168 | tf_op jit(solution)/shard_map/dynamic_slice | solution.py:607
  13.9 3.6 %collective-permute-start.2 = (bf16[64,2048]{1,0:T(8,128)(2,1)}, bf16[64,2048]{1,0:T(8,128)(2,1)S(1)}, u32[]{:S(2)}, u32[]{:S(2)}) collective-permute-start(bf16[64,2048]{1,0:T(8,128)(2,1)} %get-tuple-element.49), channel_id=1, source_target_pairs={{0,3},{1,0},{2,1},{3,2},{4,7},{5,4},{6,5},{7,6},{8,11},{9,8},{10,9... | collective-permute-start | bytes 786440 | tf_op jit(solution)/shard_map/ppermute | solution.py:609
  17.5 0.0 collective-permute-start
  17.5 1.0 collective-permute-start.1
  18.5 6.0 %collective-permute-done.2.refs_3_ = bf16[64,2048]{1,0:T(8,128)(2,1)S(1)} collective-permute-done((bf16[64,2048]{1,0:T(8,128)(2,1)}, bf16[64,2048]{1,0:T(8,128)(2,1)S(1)}, u32[]{:S(2)}, u32[]{:S(2)}) %collective-permute-start.2) | collective-permute-done | bytes 262176 | tf_op jit(solution)/shard_map/ppermute | solution.py:609
  24.6 0.0 collective-permute-start.5
  24.6 6.6 %collective-permute-done.refs_1_ = bf16[64,2048]{1,0:T(8,128)(2,1)} collective-permute-done((bf16[64,2048]{1,0:T(8,128)(2,1)}, bf16[64,2048]{1,0:T(8,128)(2,1)}, u32[]{:S(2)}, u32[]{:S(2)}) %collective-permute-start) | collective-permute-done | bytes 262176 | tf_op jit(solution)/shard_map/ppermute | solution.py:609
  31.1 1.5 collective-permute-start.6
  32.6 7.8 %collective-permute-done.1.refs_2_ = bf16[64,2048]{1,0:T(8,128)(2,1)} collective-permute-done((bf16[64,2048]{1,0:T(8,128)(2,1)}, bf16[64,2048]{1,0:T(8,128)(2,1)}, u32[]{:S(2)}, u32[]{:S(2)}) %collective-permute-start.1) | collective-permute-done | bytes 262176 | tf_op jit(solution)/shard_map/ppermute | solution.py:609
  40.4 0.3 collective-permute-start.7
  40.7 0.0 collective-permute-done.3.refs_1_
  40.7 1.2 collective-permute-start.8
  41.9 1.3 collective-permute-done.4.refs_2_
  43.3 1.0 collective-permute-start.9
  44.2 0.1 constant_dynamic-slice_fusion.4
  44.3 0.7 reshape.22.own_ref
  44.9 0.5 and_select_fusion.source_ref
  45.4 12.2 %filter_spectrum.1.refs_4_.refs_2_ = f32[8,512,256]{2,1,0:T(8,128)} custom-call(f32[256,2048]{1,0:T(8,128)} %filters_ref.1, bf16[8,512,512]{2,1,0:T(8,128)(2,1)} %constant.151.clone.fh_ref.refs_3_, bf16[8,512,512]{2,1,0:T(8,128)(2,1)} %constant.152.clone.fl_ref, bf16[128,2048]{1,0:T(8,128)(2,1)} %get-tuple-element.27.after_ref.refs_0_), custom_call_target="tpu_custom_call" | custom-call | flops 3221225472 | bytes 18874368 | tf_op jit(solution)/shard_map/filter_spectrum/pallas_call | solution.py:385
  57.7 0.0 all-to-all-done
  57.7 0.0 copy-start
  57.7 1.3 copy-done
  59.0 4.6 %settle_query.1 = (bf16[256,2048]{1,0:T(8,128)(2,1)}, bf16[256,2048]{1,0:T(8,128)(2,1)}, bf16[8,256,256]{2,1,0:T(8,128)(2,1)}) custom-call(s32[4]{0:T(128)} %and_select_fusion.source_ref, s32[1,512]{1,0:T(1,128)} %reshape.22.own_ref, bf16[512,2048]{1,0:T(8,128)(2,1)} %bitcast.4, bf16[64,2048]{1,0:T(8,128)(2,1)} %get-tuple-element.51.refs_0_, ...), custom_call_target="tpu_custom_call" | custom-call | flops 536870912 | bytes 6291456 | tf_op jit(solution)/shard_map/settle_query/pallas_call | solution.py:541
  63.6 0.0 collective-permute-done.5.refs_3_
  63.6 0.0 collective-permute-done.6.refs_4_
  63.6 12.4 %collective-permute-done.7.refs_5_ = bf16[128,2048]{1,0:T(8,128)(2,1)} collective-permute-done((bf16[128,2048]{1,0:T(8,128)(2,1)}, bf16[128,2048]{1,0:T(8,128)(2,1)}, u32[]{:S(2)}, u32[]{:S(2)}) %collective-permute-start.7) | collective-permute-done | bytes 524320 | tf_op jit(solution)/shard_map/ppermute | solution.py:579
  75.9 0.0 collective-permute-done.8.refs_6_
  75.9 1.2 collective-permute-done.9.refs_7_
  77.1 3.6 %all-to-all-start.2 = ((bf16[8,256,256]{2,1,0:T(8,128)(2,1)}), bf16[8,256,256]{2,1,0:T(8,128)(2,1)S(1)}, u32[]{:S(2)}, u32[]{:S(2)}) async-start(bf16[8,256,256]{2,1,0:T(8,128)(2,1)} %gate.1.after_ref), calls=%async_computation.2 | async-start | bytes 2097152 | tf_op jit(solution)/shard_map/all_to_all | solution.py:586
  80.8 0.1 fusion.1
  80.9 0.7 concatenate.3.own_ref
  81.5 5.3 %settle_signal.1 = (bf16[256,2048]{1,0:T(8,128)(2,1)}, bf16[256,2048]{1,0:T(8,128)(2,1)}, bf16[8,256,256]{2,1,0:T(8,128)(2,1)}) custom-call(s32[1]{0:T(128)} %bitcast.turn_ref, s32[1,512]{1,0:T(1,128)} %concatenate.3.own_ref, bf16[8,256,256]{2,1,0:T(8,128)(2,1)} %gate.1.after_ref, bf16[128,2048]{1,0:T(8,128)(2,1)} %get-tuple-element.27.after_ref.refs_0_, ...), custom_call_target="tpu_custom_call" | custom-call | flops 1073741824 | bytes 7340032 | tf_op jit(solution)/shard_map/settle_signal/pallas_call | solution.py:520
  86.8 9.2 %all-to-all-done.2.refs_0_ = bf16[8,256,256]{2,1,0:T(8,128)(2,1)S(1)} async-done(((bf16[8,256,256]{2,1,0:T(8,128)(2,1)}), bf16[8,256,256]{2,1,0:T(8,128)(2,1)S(1)}, u32[]{:S(2)}, u32[]{:S(2)}) %all-to-all-start.2) | async-done | bytes 1048608 | tf_op jit(solution)/shard_map/all_to_all | solution.py:586
  96.0 3.6 %all-to-all-start.1 = ((bf16[8,256,256]{2,1,0:T(8,128)(2,1)}), bf16[8,256,256]{2,1,0:T(8,128)(2,1)S(1)}, u32[]{:S(2)}, u32[]{:S(2)}) async-start(bf16[8,256,256]{2,1,0:T(8,128)(2,1)} %get-tuple-element.36.refs_5_), calls=%async_computation.1 | async-start | bytes 2097152 | tf_op jit(solution)/shard_map/all_to_all | solution.py:586
  99.6 12.9 %convolve_backward.1 = (bf16[8,256,256]{2,1,0:T(8,128)(2,1)}, f32[8,512,256]{2,1,0:T(8,128)}) custom-call(s32[1]{0:T(128)} %bitcast.turn_ref, bf16[8,256,256]{2,1,0:T(8,128)(2,1)} %copy-done.1, f32[1,256]{1,0:T(1,128)} %bitcast.6, f32[8,512,256]{2,1,0:T(8,128)} %filter_spectrum.1.refs_4_.refs_2_, bf16[8,512,512]{2,1,0:T(8,128)(2,1)} %constant.151.clone.fh_ref.refs_3_, ...), custom_call_target="tpu_custom_call" | custom-call | flops 2147483648 | bytes 20971520 | tf_op jit(solution)/shard_map/convolve_backward/pallas_call | solution.py:410
  112.5 2.4 %all-to-all-done.1.refs_0_ = bf16[8,256,256]{2,1,0:T(8,128)(2,1)S(1)} async-done(((bf16[8,256,256]{2,1,0:T(8,128)(2,1)}), bf16[8,256,256]{2,1,0:T(8,128)(2,1)S(1)}, u32[]{:S(2)}, u32[]{:S(2)}) %all-to-all-start.1) | async-done | bytes 1048608 | tf_op jit(solution)/shard_map/all_to_all | solution.py:586
  114.9 3.7 %all-to-all-start.4 = ((bf16[8,256,256]{2,1,0:T(8,128)(2,1)}), bf16[8,256,256]{2,1,0:T(8,128)(2,1)S(1)}, u32[]{:S(2)}, u32[]{:S(2)}) async-start(bf16[8,256,256]{2,1,0:T(8,128)(2,1)} %get-tuple-element.37.refs_5_), calls=%async_computation.4 | async-start | bytes 2097152 | tf_op jit(solution)/shard_map/all_to_all | solution.py:586
  118.7 12.8 %convolve_forward.1 = (bf16[8,256,256]{2,1,0:T(8,128)(2,1)}, f32[8,512,256]{2,1,0:T(8,128)}) custom-call(s32[1]{0:T(128)} %bitcast.turn_ref, bf16[8,256,256]{2,1,0:T(8,128)(2,1)} %copy-done.3, f32[1,256]{1,0:T(1,128)} %bitcast.7, f32[8,512,256]{2,1,0:T(8,128)} %filter_spectrum.1.refs_4_.refs_2_, bf16[8,512,512]{2,1,0:T(8,128)(2,1)} %constant.151.clone.fh_ref.refs_3_, ...), custom_call_target="tpu_custom_call" | custom-call | flops 2147483648 | bytes 20971520 | tf_op jit(solution)/shard_map/convolve_forward/pallas_call | solution.py:410
  131.5 2.3 %all-to-all-done.4.shared_ref = bf16[8,256,256]{2,1,0:T(8,128)(2,1)S(1)} async-done(((bf16[8,256,256]{2,1,0:T(8,128)(2,1)}), bf16[8,256,256]{2,1,0:T(8,128)(2,1)S(1)}, u32[]{:S(2)}, u32[]{:S(2)}) %all-to-all-start.4) | async-done | bytes 1048608 | tf_op jit(solution)/shard_map/all_to_all | solution.py:586
  133.9 3.6 %all-to-all-start.3 = ((bf16[8,256,256]{2,1,0:T(8,128)(2,1)}), bf16[8,256,256]{2,1,0:T(8,128)(2,1)S(1)}, u32[]{:S(2)}, u32[]{:S(2)}) async-start(bf16[8,256,256]{2,1,0:T(8,128)(2,1)} %get-tuple-element.38), calls=%async_computation.3 | async-start | bytes 2097152 | tf_op jit(solution)/shard_map/all_to_all | solution.py:586
  137.4 10.6 %filter_gradient.1.after_ref = f32[256,2048]{1,0:T(8,128)} custom-call(f32[8,512,256]{2,1,0:T(8,128)} %get-tuple-element.43.spec_ref, f32[8,512,256]{2,1,0:T(8,128)} %get-tuple-element.44.other_ref, bf16[8,512,512]{2,1,0:T(8,128)(2,1)} %constant.153.clone.refs_4_.ih_ref), custom_call_target="tpu_custom_call" | custom-call | flops 2147483648 | bytes 16777216 | tf_op jit(solution)/shard_map/filter_gradient/pallas_call | solution.py:441
  148.1 3.0 %key_value_gradients.1 = (bf16[256,2048]{1,0:T(8,128)(2,1)}, bf16[256,2048]{1,0:T(8,128)(2,1)}) custom-call(bf16[8,256,256]{2,1,0:T(8,128)(2,1)} %copy-done.2, bf16[256,2048]{1,0:T(8,128)(2,1)} %get-tuple-element.41.a_ref, bf16[256,2048]{1,0:T(8,128)(2,1)} %get-tuple-element.42.b_ref, f32[256,2048]{1,0:T(8,128)} %filter_gradient.1.after_ref), custom_call_target="tpu_custom_call" | custom-call | flops 1048576 | bytes 5242880 | tf_op jit(solution)/shard_map/key_value_gradients/pallas_call | solution.py:560
  151.1 1.7 %all-to-all-done.3.shared_ref = bf16[8,256,256]{2,1,0:T(8,128)(2,1)S(1)} async-done(((bf16[8,256,256]{2,1,0:T(8,128)(2,1)}), bf16[8,256,256]{2,1,0:T(8,128)(2,1)S(1)}, u32[]{:S(2)}, u32[]{:S(2)}) %all-to-all-start.3) | async-done | bytes 1048608 | tf_op jit(solution)/shard_map/all_to_all | solution.py:586
  152.8 1.0 copy-done.4
  153.7 3.0 %output_and_query_gradient.1 = (bf16[256,2048]{1,0:T(8,128)(2,1)}, bf16[256,2048]{1,0:T(8,128)(2,1)}) custom-call(bf16[8,256,256]{2,1,0:T(8,128)(2,1)} %copy-done.4, bf16[256,2048]{1,0:T(8,128)(2,1)} %get-tuple-element.39.a_ref, bf16[256,2048]{1,0:T(8,128)(2,1)} %get-tuple-element.40.b_ref, bf16[256,2048]{1,0:T(8,128)(2,1)} %get-tuple-element.24.after_ref), custom_call_target="tpu_custom_call" | custom-call | flops 1048576 | bytes 5242880 | tf_op jit(solution)/shard_map/output_and_query_gradient/pallas_call | solution.py:560
  (16 shorter events, 0.0 us)
Async XLA Ops:
  0.6 57.1 %all-to-all-start = ((bf16[8,64,2048]{2,1,0:T(8,128)(2,1)}), bf16[8,64,2048]{2,1,0:T(8,128)(2,1)S(1)}, u32[]{:S(2)}, u32[]{:S(2)}) async-start(bf16[8,64,2048]{2,1,0:T(8,128)(2,1)} %bitcast.5), calls=%async_computation | async-start | bytes 4194304 | tf_op jit(solution)/shard_map/all_to_all | solution.py:586
  5.8 38.4 %copy-start.8 = (s32[8,512]{1,0:T(8,128)S(1)}, s32[8,512]{1,0:T(8,128)}, u32[]{:S(2)}) copy-start(s32[8,512]{1,0:T(8,128)} %param.13) | copy-start | bytes 49156
  9.5 31.2 %collective-permute-start.3 = (bf16[128,2048]{1,0:T(8,128)(2,1)}, bf16[128,2048]{1,0:T(8,128)(2,1)S(1)}, u32[]{:S(2)}, u32[]{:S(2)}) collective-permute-start(bf16[128,2048]{1,0:T(8,128)(2,1)} %get-tuple-element.29), channel_id=1, source_target_pairs={{0,4},{4,0},{8,12},{12,8},{16,20},{20,16},{24,28},{28,24},{1,5},{5... | collective-permute-start | bytes 1572872 | tf_op jit(solution)/shard_map/ppermute | solution.py:579
  10.1 33.2 %collective-permute-start.4 = (bf16[128,2048]{1,0:T(8,128)(2,1)}, bf16[128,2048]{1,0:T(8,128)(2,1)S(1)}, u32[]{:S(2)}, u32[]{:S(2)}) collective-permute-start(bf16[128,2048]{1,0:T(8,128)(2,1)} %get-tuple-element.30), channel_id=1, source_target_pairs={{0,8},{4,12},{8,0},{12,4},{16,24},{20,28},{24,16},{28,20},{1,9},{5... | collective-permute-start | bytes 1572872 | tf_op jit(solution)/shard_map/ppermute | solution.py:579
  13.9 10.6 %collective-permute-start.2 = (bf16[64,2048]{1,0:T(8,128)(2,1)}, bf16[64,2048]{1,0:T(8,128)(2,1)S(1)}, u32[]{:S(2)}, u32[]{:S(2)}) collective-permute-start(bf16[64,2048]{1,0:T(8,128)(2,1)} %get-tuple-element.49), channel_id=1, source_target_pairs={{0,3},{1,0},{2,1},{3,2},{4,7},{5,4},{6,5},{7,6},{8,11},{9,8},{10,9... | collective-permute-start | bytes 786440 | tf_op jit(solution)/shard_map/ppermute | solution.py:609
  17.5 13.6 %collective-permute-start = (bf16[64,2048]{1,0:T(8,128)(2,1)}, bf16[64,2048]{1,0:T(8,128)(2,1)}, u32[]{:S(2)}, u32[]{:S(2)}) collective-permute-start(bf16[64,2048]{1,0:T(8,128)(2,1)} %get-tuple-element.50), channel_id=1, source_target_pairs={{0,1},{1,2},{2,3},{3,0},{4,5},{5,6},{6,7},{7,4},{8,9},{9,10},{10,1... | collective-permute-start | bytes 786440 | tf_op jit(solution)/shard_map/ppermute | solution.py:609
  17.5 22.9 %collective-permute-start.1 = (bf16[64,2048]{1,0:T(8,128)(2,1)}, bf16[64,2048]{1,0:T(8,128)(2,1)}, u32[]{:S(2)}, u32[]{:S(2)}) collective-permute-start(bf16[64,2048]{1,0:T(8,128)(2,1)} %get-tuple-element.52), channel_id=1, source_target_pairs={{0,2},{1,3},{2,0},{3,1},{4,6},{5,7},{6,4},{7,5},{8,10},{9,11},{10,... | collective-permute-start | bytes 786440 | tf_op jit(solution)/shard_map/ppermute | solution.py:609
  24.6 33.1 %copy-start.7 = (bf16[64,2048]{1,0:T(8,128)(2,1)}, bf16[64,2048]{1,0:T(8,128)(2,1)S(1)}, u32[]{:S(2)}) copy-start(bf16[64,2048]{1,0:T(8,128)(2,1)S(1)} %collective-permute-done.2.refs_3_) | copy-start | bytes 786436
  24.6 39.0 %collective-permute-start.5 = (bf16[128,2048]{1,0:T(8,128)(2,1)}, bf16[128,2048]{1,0:T(8,128)(2,1)}, u32[]{:S(2)}, u32[]{:S(2)}) collective-permute-start(bf16[128,2048]{1,0:T(8,128)(2,1)} %get-tuple-element.31), channel_id=1, source_target_pairs={{0,12},{4,8},{8,4},{12,0},{16,28},{20,24},{24,20},{28,16},{1,13},{... | collective-permute-start | bytes 1572872 | tf_op jit(solution)/shard_map/ppermute | solution.py:579
  31.1 32.4 %collective-permute-start.6 = (bf16[128,2048]{1,0:T(8,128)(2,1)}, bf16[128,2048]{1,0:T(8,128)(2,1)}, u32[]{:S(2)}, u32[]{:S(2)}) collective-permute-start(bf16[128,2048]{1,0:T(8,128)(2,1)} %get-tuple-element.32), channel_id=1, source_target_pairs={{0,16},{4,20},{8,24},{12,28},{16,0},{20,4},{24,8},{28,12},{1,17},{... | collective-permute-start | bytes 1572872 | tf_op jit(solution)/shard_map/ppermute | solution.py:579
  40.4 35.6 %collective-permute-start.7 = (bf16[128,2048]{1,0:T(8,128)(2,1)}, bf16[128,2048]{1,0:T(8,128)(2,1)}, u32[]{:S(2)}, u32[]{:S(2)}) collective-permute-start(bf16[128,2048]{1,0:T(8,128)(2,1)} %get-tuple-element.33), channel_id=1, source_target_pairs={{0,20},{4,16},{8,28},{12,24},{16,4},{20,0},{24,12},{28,8},{1,21},{... | collective-permute-start | bytes 1572872 | tf_op jit(solution)/shard_map/ppermute | solution.py:579
  40.7 17.0 %copy-start.5 = (bf16[128,2048]{1,0:T(8,128)(2,1)}, bf16[128,2048]{1,0:T(8,128)(2,1)S(1)}, u32[]{:S(2)}) copy-start(bf16[128,2048]{1,0:T(8,128)(2,1)S(1)} %collective-permute-done.3.refs_1_) | copy-start | bytes 1572868
  40.7 35.3 %collective-permute-start.8 = (bf16[128,2048]{1,0:T(8,128)(2,1)}, bf16[128,2048]{1,0:T(8,128)(2,1)}, u32[]{:S(2)}, u32[]{:S(2)}) collective-permute-start(bf16[128,2048]{1,0:T(8,128)(2,1)} %get-tuple-element.34), channel_id=1, source_target_pairs={{0,24},{4,28},{8,16},{12,20},{16,8},{20,12},{24,0},{28,4},{1,25},{... | collective-permute-start | bytes 1572872 | tf_op jit(solution)/shard_map/ppermute | solution.py:579
  43.3 14.4 %copy-start.6 = (bf16[128,2048]{1,0:T(8,128)(2,1)}, bf16[128,2048]{1,0:T(8,128)(2,1)S(1)}, u32[]{:S(2)}) copy-start(bf16[128,2048]{1,0:T(8,128)(2,1)S(1)} %collective-permute-done.4.refs_2_) | copy-start | bytes 1572868
  43.3 33.9 %collective-permute-start.9 = (bf16[128,2048]{1,0:T(8,128)(2,1)}, bf16[128,2048]{1,0:T(8,128)(2,1)}, u32[]{:S(2)}, u32[]{:S(2)}) collective-permute-start(bf16[128,2048]{1,0:T(8,128)(2,1)} %get-tuple-element.35), channel_id=1, source_target_pairs={{0,28},{4,24},{8,20},{12,16},{16,12},{20,8},{24,4},{28,0},{1,29},{... | collective-permute-start | bytes 1572872 | tf_op jit(solution)/shard_map/ppermute | solution.py:579
  57.7 1.3 copy-start
  77.1 18.9 %all-to-all-start.2 = ((bf16[8,256,256]{2,1,0:T(8,128)(2,1)}), bf16[8,256,256]{2,1,0:T(8,128)(2,1)S(1)}, u32[]{:S(2)}, u32[]{:S(2)}) async-start(bf16[8,256,256]{2,1,0:T(8,128)(2,1)} %gate.1.after_ref), calls=%async_computation.2 | async-start | bytes 2097152 | tf_op jit(solution)/shard_map/all_to_all | solution.py:586
  96.0 3.6 %copy-start.1 = (bf16[8,256,256]{2,1,0:T(8,128)(2,1)}, bf16[8,256,256]{2,1,0:T(8,128)(2,1)S(1)}, u32[]{:S(2)}) copy-start(bf16[8,256,256]{2,1,0:T(8,128)(2,1)S(1)} %all-to-all-done.2.refs_0_) | copy-start | bytes 3145732
  96.0 18.9 %all-to-all-start.1 = ((bf16[8,256,256]{2,1,0:T(8,128)(2,1)}), bf16[8,256,256]{2,1,0:T(8,128)(2,1)S(1)}, u32[]{:S(2)}, u32[]{:S(2)}) async-start(bf16[8,256,256]{2,1,0:T(8,128)(2,1)} %get-tuple-element.36.refs_5_), calls=%async_computation.1 | async-start | bytes 2097152 | tf_op jit(solution)/shard_map/all_to_all | solution.py:586
  114.9 3.8 %copy-start.3 = (bf16[8,256,256]{2,1,0:T(8,128)(2,1)}, bf16[8,256,256]{2,1,0:T(8,128)(2,1)S(1)}, u32[]{:S(2)}) copy-start(bf16[8,256,256]{2,1,0:T(8,128)(2,1)S(1)} %all-to-all-done.1.refs_0_) | copy-start | bytes 3145732
  114.9 18.9 %all-to-all-start.4 = ((bf16[8,256,256]{2,1,0:T(8,128)(2,1)}), bf16[8,256,256]{2,1,0:T(8,128)(2,1)S(1)}, u32[]{:S(2)}, u32[]{:S(2)}) async-start(bf16[8,256,256]{2,1,0:T(8,128)(2,1)} %get-tuple-element.37.refs_5_), calls=%async_computation.4 | async-start | bytes 2097152 | tf_op jit(solution)/shard_map/all_to_all | solution.py:586
  133.9 14.2 %copy-start.2 = (bf16[8,256,256]{2,1,0:T(8,128)(2,1)}, bf16[8,256,256]{2,1,0:T(8,128)(2,1)S(1)}, u32[]{:S(2)}) copy-start(bf16[8,256,256]{2,1,0:T(8,128)(2,1)S(1)} %all-to-all-done.4.shared_ref) | copy-start | bytes 3145732
  133.9 18.9 %all-to-all-start.3 = ((bf16[8,256,256]{2,1,0:T(8,128)(2,1)}), bf16[8,256,256]{2,1,0:T(8,128)(2,1)S(1)}, u32[]{:S(2)}, u32[]{:S(2)}) async-start(bf16[8,256,256]{2,1,0:T(8,128)(2,1)} %get-tuple-element.38), calls=%async_computation.3 | async-start | bytes 2097152 | tf_op jit(solution)/shard_map/all_to_all | solution.py:586
  152.8 1.0 copy-start.4

commit v2 on v1

--- a/solution.py
+++ b/solution.py
@@ -44,7 +44,8 @@
         low = (table - high.astype(np.float32)).astype(ml_dtypes.bfloat16)
         return high, low
 
-    return parts(forward), parts(inverse)
+    tops = [(parts(table)[0][:, :span], parts(table)[0][0, span:]) for table in (forward, inverse)]
+    return parts(forward), tops
 
 
 def plus(a, b):
@@ -187,29 +188,68 @@
         shard_transform(lambda i, r, c: seq_ref[i, r, c], high_ref, low_ref)
 
     high = high_ref[slab]
-    spec_ref[0] = dot(fh_ref[0], high) + dot(fh_ref[0], low_ref[slab]) + dot(fl_ref[0], high)
-
-
-def conv_kernel(conjugate, scale, n_in, turn_ref, *refs):
+    spec = dot(fh_ref[0], high) + dot(fh_ref[0], low_ref[slab]) + dot(fl_ref[0], high)
+    spec_ref[0] = spec.astype(BF16)
+
+
+class Table:
+    def __init__(self, top_hbm, first_hbm, table_ref, sems):
+        self.top, self.first, self.table, self.sems = top_hbm, first_hbm, table_ref, sems
+        self.span = table_ref.shape[1] // 2
+
+    def copies(self, slab):
+        upper = pltpu.make_async_copy(
+            self.top.at[slab], self.table.at[slab, pl.ds(0, self.span)], self.sems.at[slab]
+        )
+        if slab > 0:
+            return [upper]
+        lower = pltpu.make_async_copy(
+            self.first, self.table.at[0, pl.ds(self.span, self.span)], self.sems.at[self.top.shape[0]]
+        )
+        return [upper, lower]
+
+    def start(self, slab):
+        for copy in self.copies(slab):
+            copy.start()
+
+    def ready(self, slab):
+        for copy in self.copies(slab):
+            copy.wait()
+        span = self.span
+        if slab > 0:
+            self.table[slab, span:, :span] = -self.table[slab, :span, span:]
+            self.table[slab, span:, span:] = self.table[slab, :span, :span]
+        return self.table[slab]
+
+
+def conv_kernel(conjugate, scale, n_in, n_out, turn_ref, *refs):
     pieces, refs = refs[:n_in], refs[n_in:]
-    bias_ref, other_hbm, fh_hbm, ih_hbm, after_ref, out_ref, spec_hbm = refs[:7]
-    fh_ref, ih_ref, other_ref, spec_ref, high_ref, slab_ref, in_sems, out_sems = refs[7:15]
-    seq_ref = pieces[0] if n_in == 1 else refs[15]
-    shards = fh_ref.shape[0]
-
-    def fetch(which, slab):
-        source, target = ((fh_hbm, fh_ref), (other_hbm, other_ref), (ih_hbm, ih_ref))[which]
-        return pltpu.make_async_copy(source.at[slab], target.at[slab], in_sems.at[which, slab])
+    bias_ref, other_hbm, ft_hbm, f0_hbm, it_hbm, i0_hbm, after_ref = refs[:7]
+    outs, refs = refs[7 : 7 + n_out], refs[7 + n_out :]
+    spec_hbm, f_ref, i_ref, other_ref, spec_ref, high_ref, slab_ref = refs[:7]
+    f_sems, i_sems, other_sems, out_sems, seq_ref, result_ref = refs[7:]
+    shards = f_ref.shape[0]
+    turn = turn_ref[0]
+    forward_table = Table(ft_hbm, f0_hbm, f_ref, f_sems)
+    inverse_table = Table(it_hbm, i0_hbm, i_ref, i_sems)
+
+    def fetch(slab):
+        return pltpu.make_async_copy(other_hbm.at[slab], other_ref.at[slab], other_sems.at[slab])
 
     def keep(slab):
         return pltpu.make_async_copy(spec_ref.at[slab], spec_hbm.at[slab], out_sems.at[slab])
 
     for slab in range(shards):
-        for which in range(3):
-            fetch(which, slab).start()
+        forward_table.start(slab)
+        fetch(slab).start()
+        inverse_table.start(slab)
     if n_in > 1:
         for number in range(n_in):
-            seq_ref[turn_ref[0] ^ number] = pieces[number][...]
+            seq_ref[turn ^ number] = pieces[number][...]
+    else:
+        seq_ref = pieces[0]
+    if n_out == 1:
+        result_ref = outs[0]
 
     def load(i, rows, lanes):
         return seq_ref[i, rows, lanes].astype(F32)
@@ -217,42 +257,58 @@
     shard_transform(load, high_ref)
 
     def forward(slab):
-        fetch(0, slab).wait()
-        spec_ref[slab] = dot(fh_ref[slab], high_ref[slab])
+        spec_ref[slab] = dot(forward_table.ready(slab), high_ref[slab])
         keep(slab).start()
 
     forward(0)
     for slab in range(shards):
         if slab + 1 < shards:
             forward(slab + 1)
-        fetch(1, slab).wait()
-        product = bin_product(spec_ref[slab], other_ref[slab], conjugate, slab == 0)
-        fetch(2, slab).wait()
-        slab_ref[slab] = dot(ih_ref[slab], product)
+        fetch(slab).wait()
+        product = bin_product(spec_ref[slab], other_ref[slab].astype(F32), conjugate, slab == 0)
+        slab_ref[slab] = dot(inverse_table.ready(slab), product)
 
     def store(i, rows, lanes, value):
         direct = bias_ref[:, lanes] * load(i, rows, lanes)
-        out_ref[i, rows, lanes] = (direct + scale * value).astype(BF16)
+        result_ref[i, rows, lanes] = (direct + scale * value).astype(BF16)
 
     shard_inverse(slab_ref, store)
+    if n_out > 1:
+        for number in range(n_out):
+            outs[number][...] = result_ref[turn ^ number]
     for slab in range(shards):
         keep(slab).wait()
 
 
-def correlation_kernel(scale, spec_ref, other_ref, ih_ref, out_ref, slab_ref, seq_ref):
-    slab = pl.program_id(0)
-    shards = pl.num_programs(0)
-    span = seq_ref.shape[1]
-    slab_ref[slab] = dot(ih_ref[0], bin_product(spec_ref[0], other_ref[0], True, slab == 0))
-
-    @pl.when(slab == shards - 1)
-    def _():
-        def store(i, rows, lanes, value):
-            seq_ref[i, rows, lanes] = scale * value
-
-        shard_inverse(slab_ref, store)
-        for i in range(seq_ref.shape[0]):
-            out_ref[:, i * span : (i + 1) * span] = seq_ref[i].T
+def correlation_kernel(
+    scale, a_hbm, b_hbm, it_hbm, i0_hbm, after_ref, out_ref, a_ref, b_ref, i_ref, slab_ref, seq_ref,
+    i_sems, spec_sems,
+):
+    shards, span = seq_ref.shape[:2]
+    inverse_table = Table(it_hbm, i0_hbm, i_ref, i_sems)
+
+    def fetch(slab):
+        return [
+            pltpu.make_async_copy(source.at[slab], target.at[slab], spec_sems.at[which, slab])
+            for which, (source, target) in enumerate(((a_hbm, a_ref), (b_hbm, b_ref)))
+        ]
+
+    for slab in range(shards):
+        for copy in fetch(slab):
+            copy.start()
+        inverse_table.start(slab)
+    for slab in range(shards):
+        for copy in fetch(slab):
+            copy.wait()
+        product = bin_product(a_ref[slab], b_ref[slab], True, slab == 0)
+        slab_ref[slab] = dot(inverse_table.ready(slab), product)
+
+    def store(i, rows, lanes, value):
+        seq_ref[i, rows, lanes] = scale * value
+
+    shard_inverse(slab_ref, store)
+    for i in range(shards):
+        out_ref[:, i * span : (i + 1) * span] = seq_ref[i].T
 
 
 def placement(own_ref, select_ref):
@@ -343,13 +399,27 @@
     by_owner(None, [out_ref], product_ref)
 
 
-def final_kernel(shared_ref, a_ref, b_ref, after_ref, a_out, b_out):
-    width = shared_ref.shape[2]
-    for part in range(shared_ref.shape[0]):
-        lanes = slice(part * width, (part + 1) * width)
-        shared = shared_ref[part].astype(F32)
-        a_out[:, lanes] = (a_ref[:, lanes].astype(F32) * shared).astype(BF16)
-        b_out[:, lanes] = (b_ref[:, lanes].astype(F32) * shared).astype(BF16)
+def final_kernel(count, turn_ref, *refs):
+    shared, (a_ref, b_ref, after_ref, a_out, b_out) = refs[:count], refs[count:]
+    width = shared[0].shape[-1]
+    parts = a_ref.shape[1] // width
+
+    def products(factor, lanes):
+        factor = factor.astype(F32)
+        a_out[:, lanes] = (a_ref[:, lanes].astype(F32) * factor).astype(BF16)
+        b_out[:, lanes] = (b_ref[:, lanes].astype(F32) * factor).astype(BF16)
+
+    if count == 1:
+        for part in range(parts):
+            products(shared[0][part], slice(part * width, (part + 1) * width))
+        return
+    for step in range(count // parts):
+
+        @pl.when(pl.program_id(0) == step)
+        def _(step=step):
+            for part in range(parts):
+                start = pl.multiple_of(((turn_ref[0] % parts) ^ part) * width, width)
+                products(shared[step * parts + part][...], pl.ds(start, width))
 
 
 def cost(flops, moved):
@@ -378,7 +448,7 @@
 
 
 def filter_spectrum(filters, tables, after):
-    (fh, fl), _ = tables
+    fh, fl = tables[0]
     width, length = filters.shape
     shards, rows, _ = fh.shape
     spec = (shards, rows, width)
@@ -387,71 +457,81 @@
         grid=(shards,),
         in_specs=[whole(filters.shape), slab_of(fh.shape), slab_of(fl.shape), UNREAD],
         out_specs=slab_of(spec),
-        out_shape=shape_of(spec, F32),
+        out_shape=shape_of(spec, BF16),
         scratch_shapes=[
             pltpu.VMEM((shards, rows // 2, width), F32),
             pltpu.VMEM(spec, BF16),
             pltpu.VMEM(spec, BF16),
         ],
         compiler_params=params(),
-        cost_estimate=cost(6 * shards * rows * rows * width, 4 * filters.size + 8 * fh.size),
+        cost_estimate=cost(1e12, 1e9),
         name="filter_spectrum",
     )(filters, fh, fl, after)
 
 
-def convolve(turn, pieces, bias, other, tables, conjugate, after):
-    (fh, _), (ih, _) = tables
-    shards, rows, _ = fh.shape
-    tokens, width = pieces[0].shape[-2:]
+def convolve(turn, pieces, bias, other, tables, conjugate, n_out, after):
+    (ft, f0), (it, i0) = tables[1]
+    shards, rows, width = other.shape
+    tokens = rows // 2
     spec = (shards, rows, width)
     seq = (shards, tokens, width)
+    out = seq if n_out == 1 else seq[1:]
     length = shards * tokens
     scale = 1.0 / (2 * length * math.sqrt(length))
-    return pl.pallas_call(
-        functools.partial(conv_kernel, conjugate, scale, len(pieces)),
+    outs = pl.pallas_call(
+        functools.partial(conv_kernel, conjugate, scale, len(pieces), n_out),
         grid_spec=pltpu.PrefetchScalarGridSpec(
             num_scalar_prefetch=1,
             grid=(1,),
-            in_specs=[whole(piece.shape) for piece in pieces] + [whole(bias.shape)] + [UNREAD] * 4,
-            out_specs=[whole(seq), UNREAD],
+            in_specs=[whole(piece.shape) for piece in pieces] + [whole(bias.shape)] + [UNREAD] * 6,
+            out_specs=[whole(out)] * n_out + [UNREAD],
             scratch_shapes=[
-                pltpu.VMEM(fh.shape, BF16),
-                pltpu.VMEM(ih.shape, BF16),
-                pltpu.VMEM(spec, F32),
+                pltpu.VMEM((shards, rows, rows), BF16),
+                pltpu.VMEM((shards, rows, rows), BF16),
+                pltpu.VMEM(spec, BF16),
                 pltpu.VMEM(spec, F32),
                 pltpu.VMEM(spec, BF16),
                 pltpu.VMEM(spec, F32),
-                pltpu.SemaphoreType.DMA((3, shards)),
+                pltpu.SemaphoreType.DMA((shards + 1,)),
+                pltpu.SemaphoreType.DMA((shards + 1,)),
                 pltpu.SemaphoreType.DMA((shards,)),
-            ]
-            + [pltpu.VMEM(seq, BF16)] * (len(pieces) > 1),
+                pltpu.SemaphoreType.DMA((shards,)),
+                pltpu.VMEM(seq, BF16),
+                pltpu.VMEM(seq, BF16),
+            ],
         ),
-        out_shape=[shape_of(seq, BF16), shape_of(spec, F32)],
+        out_shape=[shape_of(out, BF16)] * n_out + [shape_of(spec, F32)],
         compiler_params=params(),
-        cost_estimate=cost(4 * shards * rows * rows * width, 4 * fh.size + 12 * shards * rows * width),
+        cost_estimate=cost(4 * shards * rows * rows * width, 4 * ft.size + 10 * shards * rows * width),
         name="convolve_backward" if conjugate else "convolve_forward",
-    )(turn, *pieces, bias, other, fh, ih, after)
-
-
-def correlate(spec_a, spec_b, tables):
-    _, (ih, _) = tables
+    )(turn, *pieces, bias, other, ft, f0, it, i0, after)
+    return outs[:-1], outs[-1]
+
+
+def correlate(spec_a, spec_b, tables, after):
+    it, i0 = tables[1][1]
     shards, rows, width = spec_a.shape
     length = shards * rows // 2
     scale = 1.0 / (2 * length * math.sqrt(length))
     return pl.pallas_call(
         functools.partial(correlation_kernel, scale),
-        grid=(shards,),
-        in_specs=[slab_of(spec_a.shape), slab_of(spec_b.shape), slab_of(ih.shape)],
+        grid=(1,),
+        in_specs=[UNREAD] * 5,
         out_specs=whole((width, length)),
         out_shape=shape_of((width, length), F32),
         scratch_shapes=[
             pltpu.VMEM(spec_a.shape, F32),
+            pltpu.VMEM(spec_a.shape, F32),
+            pltpu.VMEM((shards, rows, rows), BF16),
+            pltpu.VMEM(spec_a.shape, F32),
             pltpu.VMEM((shards, rows // 2, width), F32),
+            pltpu.SemaphoreType.DMA((shards + 1,)),
+            pltpu.SemaphoreType.DMA((2, shards)),
         ],
         compiler_params=params(),
-        cost_estimate=cost(4 * shards * rows * rows * width, 2 * ih.size + 12 * spec_a.size),
+        cost_estimate=cost(2 * shards * rows * rows * width, 2 * it.size + 12 * spec_a.size),
         name="filter_gradient",
-    )(spec_a, spec_b, ih)
+    )(spec_a, spec_b, it, i0, after)
 
 
 def pack(turn, arrays, shards):
@@ -554,22 +634,28 @@
     )(sources, own, rows, *pieces, *after)
 
 
-def final_products(shared, a, b, after, name):
-    shards, tokens, width = shared.shape
+def final_products(turn, shared, a, b, shards, after, name):
+    tokens, width = shared[0].shape[-2:]
     _, parts, block, steps = column_plan(a.shape[1], shards, 1024)
+    pieces = len(shared) > 1
+    column_at = turned_column(tokens, block, parts, pieces)
+    if pieces:
+        shared_spec = whole((tokens, width))
+    else:
+        shared_spec = pl.BlockSpec((parts, tokens, width), lambda j, turn: (j, 0, 0))
     return pl.pallas_call(
-        final_kernel,
-        grid=(steps,),
-        in_specs=[
-            pl.BlockSpec((parts, tokens, width), lambda j: (j, 0, 0)),
-            column(tokens, block), column(tokens, block), UNREAD,
-        ],
-        out_specs=[column(tokens, block)] * 2,
+        functools.partial(final_kernel, len(shared)),
+        grid_spec=pltpu.PrefetchScalarGridSpec(
+            num_scalar_prefetch=1,
+            grid=(steps,),
+            in_specs=[shared_spec] * len(shared) + [column_at, column_at, UNREAD],
+            out_specs=[column_at, column_at],
+        ),
         out_shape=[shape_of(a.shape, BF16)] * 2,
         compiler_params=params(),
         cost_estimate=cost(2 * a.size, 10 * a.size),
         name=name,
-    )(shared, a, b, after)
+    )(turn, *shared, a, b, after)
 
 
 def permuted(pieces):
@@ -617,30 +703,31 @@
         [lax.dynamic_slice_in_dim(own, ctx_index ^ number, 1, 0) for number in range(shards)], axis=1
     )
 
-    filter_spec = filter_spectrum(filters, tables, both_packed[0])
     grad_seq, query_seq, grad_conv = settle_query(
-        own.reshape(1, slots), query_recv, grad_sources, pieces, tokens, shards, [filter_spec]
-    )
-    grad_conv = gate(grad_conv, both_slots[1:])
+        own.reshape(1, slots), query_recv, grad_sources, pieces, tokens, shards, [both_packed[0]]
+    )
     grad_recv = exchange(grad_conv)
+    filter_spec = filter_spectrum(filters, tables, grad_conv)
+    (grad_signal,), grad_spec = convolve(
+        turn, [grad_recv], bias, filter_spec, tables, True, 1, filter_spec
+    )
+    n_pieces = shards if (channels // shards) % 128 == 0 else 1
     key_seq, value_seq, signal = settle_signal(
-        turn, own_turned, both_slots, tokens, 1, grad_conv
-    )
-    signal_recv = [exchange(signal[0])]
-    grad_signal, grad_spec = convolve(
-        turn, [grad_recv], bias, filter_spec, tables, True, signal[0]
-    )
+        turn, own_turned, both_slots, tokens, n_pieces, grad_signal
+    )
+    signal_recv = permuted(signal) if n_pieces > 1 else [exchange(signal[0])]
+    grad_signal = gate(grad_signal, signal_recv)
     grad_signal_recv = exchange(grad_signal)
     conv_out, signal_spec = convolve(
-        turn, signal_recv, bias, filter_spec, tables, False, grad_signal
-    )
-    conv_recv = exchange(conv_out)
-    grad_filters = correlate(grad_spec, signal_spec, tables)
+        turn, signal_recv, bias, filter_spec, tables, False, n_pieces, grad_signal
+    )
+    conv_recv = permuted(conv_out) if n_pieces > 1 else [exchange(conv_out[0])]
+    grad_filters = correlate(grad_spec, signal_spec, tables, grad_signal_recv)
     grad_key, grad_value = final_products(
-        grad_signal_recv, value_seq, key_seq, grad_filters, "key_value_gradients"
+        turn, [grad_signal_recv], value_seq, key_seq, shards, grad_filters, "key_value_gradients"
     )
     output, grad_query = final_products(
-        conv_recv, query_seq, grad_seq, grad_key, "output_and_query_gradient"
+        turn, conv_recv, query_seq, grad_seq, shards, grad_key, "output_and_query_gradient"
     )
     return output, grad_query, grad_key, grad_value, grad_filters
 

time: 158 us -> 175 us (1.11)
  the two profiles are of different devices: /device:TPU:0 before, /device:TPU:25 now
where the time goes in v2:
time: 175 us
  Pallas kernels  68.1 us (39%)
  waiting for transfers between devices  57.9 us (33%)
  starting transfers between devices  41 us (23%)
  local copies, waits for them, and re-layouts  6.16 us (4%)
    all_to_all x3, waiting for transfers between devices, exchange(): return lax.all_to_all(value, 'ctx', split_axis=0, concat_axis=0, tiled=True)  30 us
    ppermute x21, starting transfers between devices, permuted(): lax.ppermute(pieces[number], 'ctx', [(i, i ^ number) for i in range(shard...  27.2 us
    pallas_call x2, Pallas kernels, convolve(): pl.pallas_call(functools.partial(conv_kernel, conjugate, scale, len(piece...  26.1 us
    ppermute x3, waiting for transfers between devices, per_device(): lax.ppermute(piece, 'tp', [(i, (i + shift) % tensor) for i in range(tenso...  19.3 us
    all_to_all x3, starting transfers between devices, exchange(): return lax.all_to_all(value, 'ctx', split_axis=0, concat_axis=0, tiled=True)  12.3 us
    pallas_call x1, Pallas kernels, filter_spectrum(): pl.pallas_call(filter_kernel, grid=(shards,), in_specs=[whole(filters.sha...  11.9 us
    pallas_call x1, Pallas kernels, correlate(): pl.pallas_call(functools.partial(correlation_kernel, scale), grid=(1,), i...  9.91 us
    ppermute x21, waiting for transfers between devices, permuted(): lax.ppermute(pieces[number], 'ctx', [(i, i ^ number) for i in range(shard...  8.53 us
  transfers between devices with their start and end apart: 27, of which 6 were waited for; matrix products, arithmetic and copies ran while one was open for 2% of the time, Pallas kernels for 34%

profile of v2, /device:TPU:25, one launch (start us, length us, event | category | flops | bytes accessed | tf_op | source)
XLA Modules:
  0.0 174.6 jit_solution(7416135712567569860)
XLA Ops:
  0.6 4.4 %all-to-all-start = ((bf16[8,64,2048]{2,1,0:T(8,128)(2,1)}), bf16[8,64,2048]{2,1,0:T(8,128)(2,1)S(1)}, u32[]{:S(2)}, u32[]{:S(2)}) async-start(bf16[8,64,2048]{2,1,0:T(8,128)(2,1)} %bitcast.5), calls=%async_computation | async-start | bytes 4194304 | tf_op jit(solution)/shard_map/all_to_all | solution.py:672
  5.0 3.8 %pack_rows.1 = (bf16[128,2048]{1,0:T(8,128)(2,1)}, bf16[128,2048]{1,0:T(8,128)(2,1)}, bf16[128,2048]{1,0:T(8,128)(2,1)}, bf16[128,2048]{1,0:T(8,128)(2,1)}, bf16...) custom-call(s32[1]{0:T(128)} %bitcast.turn_ref, ...), custom_call_target="tpu_custom_call" | custom-call | bytes 8388608 | tf_op jit(solution)/shard_map/pack_rows/pallas_call | solution.py:541
  8.9 1.7 collective-permute-start.4
  10.7 0.9 constant_dynamic-slice_fusion
  11.6 1.3 collective-permute-start.1
  12.9 0.2 collective-permute-start.2
  13.2 0.7 reshape.22.own_ref
  13.8 0.1 fusion.1
  13.9 0.7 concatenate.3.own_ref
  14.6 0.5 and_select_fusion.source_ref
  15.1 4.1 %collective-permute-done.refs_1_ = bf16[64,2048]{1,0:T(8,128)(2,1)S(1)} collective-permute-done((bf16[64,2048]{1,0:T(8,128)(2,1)}, bf16[64,2048]{1,0:T(8,128)(2,1)S(1)}, u32[]{:S(2)}, u32[]{:S(2)}) %collective-permute-start) | collective-permute-done | bytes 262176 | tf_op jit(solution)/shard_map/ppermute | solution.py:695
  19.2 1.5 collective-permute-start.5
  20.7 15.2 %collective-permute-done.1.refs_2_ = bf16[64,2048]{1,0:T(8,128)(2,1)S(1)} collective-permute-done((bf16[64,2048]{1,0:T(8,128)(2,1)}, bf16[64,2048]{1,0:T(8,128)(2,1)S(1)}, u32[]{:S(2)}, u32[]{:S(2)}) %collective-permute-start.1) | collective-permute-done | bytes 262176 | tf_op jit(solution)/shard_map/ppermute | solution.py:695
  35.9 1.2 collective-permute-start.6
  37.1 1.7 collective-permute-start.7
  38.9 1.3 copy-done.1
  40.2 4.6 %settle_query.1 = (bf16[256,2048]{1,0:T(8,128)(2,1)}, bf16[256,2048]{1,0:T(8,128)(2,1)}, bf16[8,256,256]{2,1,0:T(8,128)(2,1)}) custom-call(s32[4]{0:T(128)} %and_select_fusion.source_ref, s32[1,512]{1,0:T(1,128)} %reshape.22.own_ref, bf16[512,2048]{1,0:T(8,128)(2,1)} %bitcast.4, bf16[64,2048]{1,0:T(8,128)(2,1)} %get-tuple-element.79.refs_0_, ...), custom_call_target="tpu_custom_call" | custom-call | flops 536870912 | bytes 6291456 | tf_op jit(solution)/shard_map/settle_query/pallas_call | solution.py:621
  44.8 4.2 %all-to-all-start.1 = ((bf16[8,256,256]{2,1,0:T(8,128)(2,1)}), bf16[8,256,256]{2,1,0:T(8,128)(2,1)}, u32[]{:S(2)}, u32[]{:S(2)}) async-start(bf16[8,256,256]{2,1,0:T(8,128)(2,1)} %get-tuple-element.42.after_ref), calls=%async_computation.1 | async-start | bytes 2097152 | tf_op jit(solution)/shard_map/all_to_all | solution.py:672
  49.0 2.2 %collective-permute-start.8 = (bf16[128,2048]{1,0:T(8,128)(2,1)}, bf16[128,2048]{1,0:T(8,128)(2,1)}, u32[]{:S(2)}, u32[]{:S(2)}) collective-permute-start(bf16[128,2048]{1,0:T(8,128)(2,1)} %get-tuple-element.49), channel_id=1, source_target_pairs={{0,24},{4,28},{8,16},{12,20},{16,8},{20,12},{24,0},{28,4},{1,25},{... | collective-permute-start | bytes 1572872 | tf_op jit(solution)/shard_map/ppermute | solution.py:665
  51.1 0.4 collective-permute-start.9
  51.6 11.9 %filter_spectrum.1.refs_2_.refs_7_.refs_9_ = bf16[8,512,256]{2,1,0:T(8,128)(2,1)} custom-call(f32[256,2048]{1,0:T(8,128)} %filters_ref.1, bf16[8,512,512]{2,1,0:T(8,128)(2,1)} %constant.157.clone.fh_ref, bf16[8,512,512]{2,1,0:T(8,128)(2,1)} %constant.158.clone.fl_ref, bf16[8,256,256]{2,1,0:T(8,128)(2,1)} %get-tuple-element.42.after_ref), custom_call_target="tpu_custom_call" | custom-call | flops 999999995904 | bytes 1000000000 | tf_op jit(solution)/shard_map/filter_spectrum/pallas_call | solution.py:455
  63.4 30.0 %all-to-all-done.1.refs_0_ = bf16[8,256,256]{2,1,0:T(8,128)(2,1)} async-done(((bf16[8,256,256]{2,1,0:T(8,128)(2,1)}), bf16[8,256,256]{2,1,0:T(8,128)(2,1)}, u32[]{:S(2)}, u32[]{:S(2)}) %all-to-all-start.1) | async-done | bytes 1048608 | tf_op jit(solution)/shard_map/all_to_all | solution.py:672
  93.5 13.0 %convolve_backward.1 = (bf16[8,256,256]{2,1,0:T(8,128)(2,1)}, f32[8,512,256]{2,1,0:T(8,128)}) custom-call(s32[1]{0:T(128)} %bitcast.turn_ref, bf16[8,256,256]{2,1,0:T(8,128)(2,1)} %all-to-all-done.1.refs_0_, f32[1,256]{1,0:T(1,128)} %bitcast.6, bf16[8,512,256]{2,1,0:T(8,128)(2,1)} %filter_spectrum.1.refs_2_.refs_7_.refs_9_, ...), custom_call_target="tpu_custom_call" | custom-call | flops 2147483648 | bytes 14680064 | tf_op jit(solution)/shard_map/convolve_backward/pallas_call | solution.py:481
  106.5 5.7 %settle_signal.1 = (bf16[256,2048]{1,0:T(8,128)(2,1)}, bf16[256,2048]{1,0:T(8,128)(2,1)}, bf16[256,256]{1,0:T(8,128)(2,1)}, bf16[256,256]{1,0:T(8,128)(2,1)}, bf...) custom-call(s32[1]{0:T(128)} %bitcast.turn_ref, ...), custom_call_target="tpu_custom_call" | custom-call | flops 1073741824 | bytes 7340032 | tf_op jit(solution)/shard_map/settle_signal/pallas_call | solution.py:600
  112.2 2.2 %collective-permute-start.10 = (bf16[256,256]{1,0:T(8,128)(2,1)}, bf16[256,256]{1,0:T(8,128)(2,1)S(1)}, u32[]{:S(2)}, u32[]{:S(2)}) collective-permute-start(bf16[256,256]{1,0:T(8,128)(2,1)} %get-tuple-element.52), channel_id=1, source_target_pairs={{0,4},{4,0},{8,12},{12,8},{16,20},{20,16},{24,28},{28,24},{1,5},{5... | collective-permute-start | bytes 393224 | tf_op jit(solution)/shard_map/ppermute | solution.py:665
  114.4 1.7 collective-permute-start.12
  116.1 1.2 collective-permute-start.13
  117.3 0.6 collective-permute-start.14
  117.9 1.2 collective-permute-start.15
  119.1 0.6 collective-permute-done.11.refs_3_.refs_2_
  119.7 2.4 %collective-permute-start.16 = (bf16[256,256]{1,0:T(8,128)(2,1)}, bf16[256,256]{1,0:T(8,128)(2,1)S(1)}, u32[]{:S(2)}, u32[]{:S(2)}) collective-permute-start(bf16[256,256]{1,0:T(8,128)(2,1)} %get-tuple-element.58), channel_id=1, source_target_pairs={{0,28},{4,24},{8,20},{12,16},{16,12},{20,8},{24,4},{28,0},{1,29},{... | collective-permute-start | bytes 393224 | tf_op jit(solution)/shard_map/ppermute | solution.py:665
  122.0 1.3 collective-permute-done.12.refs_4_.refs_3_
  123.4 6.6 %collective-permute-done.14.refs_6_.refs_5_ = bf16[256,256]{1,0:T(8,128)(2,1)S(1)} collective-permute-done((bf16[256,256]{1,0:T(8,128)(2,1)}, bf16[256,256]{1,0:T(8,128)(2,1)S(1)}, u32[]{:S(2)}, u32[]{:S(2)}) %collective-permute-start.14) | collective-permute-done | bytes 131104 | tf_op jit(solution)/shard_map/ppermute | solution.py:665
  130.0 0.6 copy-done.7
  130.7 3.7 %all-to-all-start.2 = ((bf16[8,256,256]{2,1,0:T(8,128)(2,1)}), bf16[8,256,256]{2,1,0:T(8,128)(2,1)S(1)}, u32[]{:S(2)}, u32[]{:S(2)}) async-start(bf16[8,256,256]{2,1,0:T(8,128)(2,1)} %gate.1.refs_14_), calls=%async_computation.2 | async-start | bytes 2097152 | tf_op jit(solution)/shard_map/all_to_all | solution.py:672
  134.4 13.2 %convolve_forward.1 = (bf16[256,256]{1,0:T(8,128)(2,1)}, bf16[256,256]{1,0:T(8,128)(2,1)}, bf16[256,256]{1,0:T(8,128)(2,1)}, bf16[256,256]{1,0:T(8,128)(2,1)}, b...) custom-call(s32[1]{0:T(128)} %bitcast.turn_ref, ...), custom_call_target="tpu_custom_call" | custom-call | flops 2147483648 | bytes 14680064 | tf_op jit(solution)/shard_map/convolve_forward/pallas_call | solution.py:481
  147.5 0.2 collective-permute-start.17
  147.8 1.4 collective-permute-start.18
  149.2 0.5 collective-permute-start.19
  149.8 1.3 collective-permute-start.20
  151.0 0.3 collective-permute-start.21
  151.3 2.3 %collective-permute-start.22 = (bf16[256,256]{1,0:T(8,128)(2,1)}, bf16[256,256]{1,0:T(8,128)(2,1)S(1)}, u32[]{:S(2)}, u32[]{:S(2)}) collective-permute-start(bf16[256,256]{1,0:T(8,128)(2,1)} %get-tuple-element.65), channel_id=1, source_target_pairs={{0,24},{4,28},{8,16},{12,20},{16,8},{20,12},{24,0},{28,4},{1,25},{... | collective-permute-start | bytes 393224 | tf_op jit(solution)/shard_map/ppermute | solution.py:665
  153.7 3.1 %collective-permute-start.23 = (bf16[256,256]{1,0:T(8,128)(2,1)}, bf16[256,256]{1,0:T(8,128)(2,1)S(1)}, u32[]{:S(2)}, u32[]{:S(2)}) collective-permute-start(bf16[256,256]{1,0:T(8,128)(2,1)} %get-tuple-element.66), channel_id=1, source_target_pairs={{0,28},{4,24},{8,20},{12,16},{16,12},{20,8},{24,4},{28,0},{1,29},{... | collective-permute-start | bytes 393224 | tf_op jit(solution)/shard_map/ppermute | solution.py:665
  156.7 1.0 copy-done
  157.7 9.9 %filter_gradient.1.refs_3_ = f32[256,2048]{1,0:T(8,128)} custom-call(f32[8,512,256]{2,1,0:T(8,128)} %get-tuple-element.71.a_hbm, f32[8,512,256]{2,1,0:T(8,128)} %get-tuple-element.72.b_hbm, bf16[8,256,512]{2,1,0:T(8,128)(2,1)} %constant.161.clone.refs_5_.refs_12_.it_hbm, bf16[256,512]{1,0:T(8,128)(2,1)} %constant.162.clone.refs_6_.refs_13_.i0_hbm, ...), custom_call_target="tpu_custom_call" | custom-call | flops 1073741824 | bytes 14680064 | tf_op jit(solution)/shard_map/filter_gradient/pallas_call | solution.py:516
  167.6 3.0 %key_value_gradients.1 = (bf16[256,2048]{1,0:T(8,128)(2,1)}, bf16[256,2048]{1,0:T(8,128)(2,1)}) custom-call(s32[1]{0:T(128)} %bitcast.turn_ref, bf16[8,256,256]{2,1,0:T(8,128)(2,1)} %copy-done, bf16[256,2048]{1,0:T(8,128)(2,1)} %get-tuple-element.69.refs_1_, bf16[256,2048]{1,0:T(8,128)(2,1)} %get-tuple-element.70.refs_2_, f32[256,2048]{1,0:T(8,128)} %filter_gradient.1.refs_3_), custom_call_target="tpu_custom_call" | custom-call | flops 1048576 | bytes 5242880 | tf_op jit(solution)/shard_map/key_value_gradients/pallas_call | solution.py:646
  170.8 0.6 copy-done.15
  171.5 3.1 %output_and_query_gradient.1 = (bf16[256,2048]{1,0:T(8,128)(2,1)}, bf16[256,2048]{1,0:T(8,128)(2,1)}) custom-call(s32[1]{0:T(128)} %bitcast.turn_ref, bf16[256,256]{1,0:T(8,128)(2,1)} %get-tuple-element.59.refs_0_, bf16[256,256]{1,0:T(8,128)(2,1)} %copy-done.13, bf16[256,256]{1,0:T(8,128)(2,1)} %copy-done.14, bf16[256,256]{1,0:T(8,128)(2,1)} %copy-done.15, ...), custom_call_target="tpu_custom_call" | custom-call | flops 1048576 | bytes 5242880 | tf_op jit(solution)/shard_map/output_and_query_gradient/pallas_call | solution.py:646
  (64 shorter events, 0.6 us)
Async XLA Ops:
  0.6 38.2 %all-to-all-start = ((bf16[8,64,2048]{2,1,0:T(8,128)(2,1)}), bf16[8,64,2048]{2,1,0:T(8,128)(2,1)S(1)}, u32[]{:S(2)}, u32[]{:S(2)}) async-start(bf16[8,64,2048]{2,1,0:T(8,128)(2,1)} %bitcast.5), calls=%async_computation | async-start | bytes 4194304 | tf_op jit(solution)/shard_map/all_to_all | solution.py:672
  5.0 5.6 %copy-start.2 = (bf16[64,8192]{1,0:T(8,128)(2,1)S(1)}, bf16[64,8192]{1,0:T(8,128)(2,1)}, u32[]{:S(2)}) copy-start(bf16[64,8192]{1,0:T(8,128)(2,1)} %param.19) | copy-start | bytes 3145732
  8.8 4.2 %copy-start.20 = (s32[8,512]{1,0:T(8,128)S(1)}, s32[8,512]{1,0:T(8,128)}, u32[]{:S(2)}) copy-start(s32[8,512]{1,0:T(8,128)} %param.16) | copy-start | bytes 49156
  8.9 40.1 %collective-permute-start.3 = (bf16[128,2048]{1,0:T(8,128)(2,1)}, bf16[128,2048]{1,0:T(8,128)(2,1)}, u32[]{:S(2)}, u32[]{:S(2)}) collective-permute-start(bf16[128,2048]{1,0:T(8,128)(2,1)} %get-tuple-element.44), channel_id=1, source_target_pairs={{0,4},{4,0},{8,12},{12,8},{16,20},{20,16},{24,28},{28,24},{1,5},{5... | collective-permute-start | bytes 1572872 | tf_op jit(solution)/shard_map/ppermute | solution.py:665
  8.9 42.2 %collective-permute-start.4 = (bf16[128,2048]{1,0:T(8,128)(2,1)}, bf16[128,2048]{1,0:T(8,128)(2,1)}, u32[]{:S(2)}, u32[]{:S(2)}) collective-permute-start(bf16[128,2048]{1,0:T(8,128)(2,1)} %get-tuple-element.45), channel_id=1, source_target_pairs={{0,8},{4,12},{8,0},{12,4},{16,24},{20,28},{24,16},{28,20},{1,9},{5... | collective-permute-start | bytes 1572872 | tf_op jit(solution)/shard_map/ppermute | solution.py:665
  11.6 7.6 %collective-permute-start = (bf16[64,2048]{1,0:T(8,128)(2,1)}, bf16[64,2048]{1,0:T(8,128)(2,1)S(1)}, u32[]{:S(2)}, u32[]{:S(2)}) collective-permute-start(bf16[64,2048]{1,0:T(8,128)(2,1)} %get-tuple-element.78), channel_id=1, source_target_pairs={{0,1},{1,2},{2,3},{3,0},{4,5},{5,6},{6,7},{7,4},{8,9},{9,10},{10,1... | collective-permute-start | bytes 786440 | tf_op jit(solution)/shard_map/ppermute | solution.py:695
  11.6 24.4 %collective-permute-start.1 = (bf16[64,2048]{1,0:T(8,128)(2,1)}, bf16[64,2048]{1,0:T(8,128)(2,1)S(1)}, u32[]{:S(2)}, u32[]{:S(2)}) collective-permute-start(bf16[64,2048]{1,0:T(8,128)(2,1)} %get-tuple-element.80), channel_id=1, source_target_pairs={{0,2},{1,3},{2,0},{3,1},{4,6},{5,7},{6,4},{7,5},{8,10},{9,11},{10,... | collective-permute-start | bytes 786440 | tf_op jit(solution)/shard_map/ppermute | solution.py:695
  12.9 24.2 %collective-permute-start.2 = (bf16[64,2048]{1,0:T(8,128)(2,1)S(1)}, bf16[64,2048]{1,0:T(8,128)(2,1)S(1)}, u32[]{:S(2)}, u32[]{:S(2)}) collective-permute-start(bf16[64,2048]{1,0:T(8,128)(2,1)S(1)} %get-tuple-element.77), channel_id=1, source_target_pairs={{0,3},{1,0},{2,1},{3,2},{4,7},{5,4},{6,5},{7,6},{8,11},{9,8},{10,9... | collective-permute-start | bytes 786440 | tf_op jit(solution)/shard_map/ppermute | solution.py:695
  19.2 19.7 %copy-start.10 = (bf16[64,2048]{1,0:T(8,128)(2,1)}, bf16[64,2048]{1,0:T(8,128)(2,1)S(1)}, u32[]{:S(2)}) copy-start(bf16[64,2048]{1,0:T(8,128)(2,1)S(1)} %collective-permute-done.refs_1_) | copy-start | bytes 786436
  19.2 87.2 %collective-permute-start.5 = (bf16[128,2048]{1,0:T(8,128)(2,1)}, bf16[128,2048]{1,0:T(8,128)(2,1)}, u32[]{:S(2)}, u32[]{:S(2)}) collective-permute-start(bf16[128,2048]{1,0:T(8,128)(2,1)} %get-tuple-element.46), channel_id=1, source_target_pairs={{0,12},{4,8},{8,4},{12,0},{16,28},{20,24},{24,20},{28,16},{1,13},{... | collective-permute-start | bytes 1572872 | tf_op jit(solution)/shard_map/ppermute | solution.py:665
  35.9 2.9 %copy-start.11 = (bf16[64,2048]{1,0:T(8,128)(2,1)}, bf16[64,2048]{1,0:T(8,128)(2,1)S(1)}, u32[]{:S(2)}) copy-start(bf16[64,2048]{1,0:T(8,128)(2,1)S(1)} %collective-permute-done.1.refs_2_) | copy-start | bytes 786436
  35.9 70.5 %collective-permute-start.6 = (bf16[128,2048]{1,0:T(8,128)(2,1)}, bf16[128,2048]{1,0:T(8,128)(2,1)}, u32[]{:S(2)}, u32[]{:S(2)}) collective-permute-start(bf16[128,2048]{1,0:T(8,128)(2,1)} %get-tuple-element.47), channel_id=1, source_target_pairs={{0,16},{4,20},{8,24},{12,28},{16,0},{20,4},{24,8},{28,12},{1,17},{... | collective-permute-start | bytes 1572872 | tf_op jit(solution)/shard_map/ppermute | solution.py:665
  37.1 1.7 %copy-start.12 = (bf16[64,2048]{1,0:T(8,128)(2,1)}, bf16[64,2048]{1,0:T(8,128)(2,1)S(1)}, u32[]{:S(2)}) copy-start(bf16[64,2048]{1,0:T(8,128)(2,1)S(1)} %collective-permute-done.2.refs_3_) | copy-start | bytes 786436
  37.1 69.3 %collective-permute-start.7 = (bf16[128,2048]{1,0:T(8,128)(2,1)}, bf16[128,2048]{1,0:T(8,128)(2,1)}, u32[]{:S(2)}, u32[]{:S(2)}) collective-permute-start(bf16[128,2048]{1,0:T(8,128)(2,1)} %get-tuple-element.48), channel_id=1, source_target_pairs={{0,20},{4,16},{8,28},{12,24},{16,4},{20,0},{24,12},{28,8},{1,21},{... | collective-permute-start | bytes 1572872 | tf_op jit(solution)/shard_map/ppermute | solution.py:665
  38.9 1.3 copy-start.1
  44.8 48.7 %all-to-all-start.1 = ((bf16[8,256,256]{2,1,0:T(8,128)(2,1)}), bf16[8,256,256]{2,1,0:T(8,128)(2,1)}, u32[]{:S(2)}, u32[]{:S(2)}) async-start(bf16[8,256,256]{2,1,0:T(8,128)(2,1)} %get-tuple-element.42.after_ref), calls=%async_computation.1 | async-start | bytes 2097152 | tf_op jit(solution)/shard_map/all_to_all | solution.py:672
  49.0 57.5 %collective-permute-start.8 = (bf16[128,2048]{1,0:T(8,128)(2,1)}, bf16[128,2048]{1,0:T(8,128)(2,1)}, u32[]{:S(2)}, u32[]{:S(2)}) collective-permute-start(bf16[128,2048]{1,0:T(8,128)(2,1)} %get-tuple-element.49), channel_id=1, source_target_pairs={{0,24},{4,28},{8,16},{12,20},{16,8},{20,12},{24,0},{28,4},{1,25},{... | collective-permute-start | bytes 1572872 | tf_op jit(solution)/shard_map/ppermute | solution.py:665
  51.1 55.3 %collective-permute-start.9 = (bf16[128,2048]{1,0:T(8,128)(2,1)}, bf16[128,2048]{1,0:T(8,128)(2,1)}, u32[]{:S(2)}, u32[]{:S(2)}) collective-permute-start(bf16[128,2048]{1,0:T(8,128)(2,1)} %get-tuple-element.50), channel_id=1, source_target_pairs={{0,28},{4,24},{8,20},{12,16},{16,12},{20,8},{24,4},{28,0},{1,29},{... | collective-permute-start | bytes 1572872 | tf_op jit(solution)/shard_map/ppermute | solution.py:665
  112.2 5.7 %collective-permute-start.10 = (bf16[256,256]{1,0:T(8,128)(2,1)}, bf16[256,256]{1,0:T(8,128)(2,1)S(1)}, u32[]{:S(2)}, u32[]{:S(2)}) collective-permute-start(bf16[256,256]{1,0:T(8,128)(2,1)} %get-tuple-element.52), channel_id=1, source_target_pairs={{0,4},{4,0},{8,12},{12,8},{16,20},{20,16},{24,28},{28,24},{1,5},{5... | collective-permute-start | bytes 393224 | tf_op jit(solution)/shard_map/ppermute | solution.py:665
  114.4 5.3 %collective-permute-start.11 = (bf16[256,256]{1,0:T(8,128)(2,1)}, bf16[256,256]{1,0:T(8,128)(2,1)S(1)}, u32[]{:S(2)}, u32[]{:S(2)}) collective-permute-start(bf16[256,256]{1,0:T(8,128)(2,1)} %get-tuple-element.53), channel_id=1, source_target_pairs={{0,8},{4,12},{8,0},{12,4},{16,24},{20,28},{24,16},{28,20},{1,9},{5... | collective-permute-start | bytes 393224 | tf_op jit(solution)/shard_map/ppermute | solution.py:665
  114.4 9.0 %collective-permute-start.12 = (bf16[256,256]{1,0:T(8,128)(2,1)}, bf16[256,256]{1,0:T(8,128)(2,1)S(1)}, u32[]{:S(2)}, u32[]{:S(2)}) collective-permute-start(bf16[256,256]{1,0:T(8,128)(2,1)} %get-tuple-element.54), channel_id=1, source_target_pairs={{0,12},{4,8},{8,4},{12,0},{16,28},{20,24},{24,20},{28,16},{1,13},{... | collective-permute-start | bytes 393224 | tf_op jit(solution)/shard_map/ppermute | solution.py:665
  116.1 7.3 %collective-permute-start.13 = (bf16[256,256]{1,0:T(8,128)(2,1)}, bf16[256,256]{1,0:T(8,128)(2,1)S(1)}, u32[]{:S(2)}, u32[]{:S(2)}) collective-permute-start(bf16[256,256]{1,0:T(8,128)(2,1)} %get-tuple-element.55), channel_id=1, source_target_pairs={{0,16},{4,20},{8,24},{12,28},{16,0},{20,4},{24,8},{28,12},{1,17},{... | collective-permute-start | bytes 393224 | tf_op jit(solution)/shard_map/ppermute | solution.py:665
  117.3 12.7 %collective-permute-start.14 = (bf16[256,256]{1,0:T(8,128)(2,1)}, bf16[256,256]{1,0:T(8,128)(2,1)S(1)}, u32[]{:S(2)}, u32[]{:S(2)}) collective-permute-start(bf16[256,256]{1,0:T(8,128)(2,1)} %get-tuple-element.56), channel_id=1, source_target_pairs={{0,20},{4,16},{8,28},{12,24},{16,4},{20,0},{24,12},{28,8},{1,21},{... | collective-permute-start | bytes 393224 | tf_op jit(solution)/shard_map/ppermute | solution.py:665
  117.9 12.1 %copy-start.3 = (bf16[256,256]{1,0:T(8,128)(2,1)}, bf16[256,256]{1,0:T(8,128)(2,1)S(1)}, u32[]{:S(2)}) copy-start(bf16[256,256]{1,0:T(8,128)(2,1)S(1)} %collective-permute-done.10.refs_2_.refs_1_) | copy-start | bytes 393220
  117.9 12.1 %collective-permute-start.15 = (bf16[256,256]{1,0:T(8,128)(2,1)}, bf16[256,256]{1,0:T(8,128)(2,1)S(1)}, u32[]{:S(2)}, u32[]{:S(2)}) collective-permute-start(bf16[256,256]{1,0:T(8,128)(2,1)} %get-tuple-element.57), channel_id=1, source_target_pairs={{0,24},{4,28},{8,16},{12,20},{16,8},{20,12},{24,0},{28,4},{1,25},{... | collective-permute-start | bytes 393224 | tf_op jit(solution)/shard_map/ppermute | solution.py:665
  119.7 10.3 %copy-start.4 = (bf16[256,256]{1,0:T(8,128)(2,1)}, bf16[256,256]{1,0:T(8,128)(2,1)S(1)}, u32[]{:S(2)}) copy-start(bf16[256,256]{1,0:T(8,128)(2,1)S(1)} %collective-permute-done.11.refs_3_.refs_2_) | copy-start | bytes 393220
  119.7 10.3 %collective-permute-start.16 = (bf16[256,256]{1,0:T(8,128)(2,1)}, bf16[256,256]{1,0:T(8,128)(2,1)S(1)}, u32[]{:S(2)}, u32[]{:S(2)}) collective-permute-start(bf16[256,256]{1,0:T(8,128)(2,1)} %get-tuple-element.58), channel_id=1, source_target_pairs={{0,28},{4,24},{8,20},{12,16},{16,12},{20,8},{24,4},{28,0},{1,29},{... | collective-permute-start | bytes 393224 | tf_op jit(solution)/shard_map/ppermute | solution.py:665
  123.4 6.6 %copy-start.5 = (bf16[256,256]{1,0:T(8,128)(2,1)}, bf16[256,256]{1,0:T(8,128)(2,1)S(1)}, u32[]{:S(2)}) copy-start(bf16[256,256]{1,0:T(8,128)(2,1)S(1)} %collective-permute-done.12.refs_4_.refs_3_) | copy-start | bytes 393220
  123.4 6.6 %copy-start.6 = (bf16[256,256]{1,0:T(8,128)(2,1)}, bf16[256,256]{1,0:T(8,128)(2,1)S(1)}, u32[]{:S(2)}) copy-start(bf16[256,256]{1,0:T(8,128)(2,1)S(1)} %collective-permute-done.13.refs_5_.refs_4_) | copy-start | bytes 393220
  129.9 0.6 copy-start.7
  129.9 0.7 copy-start.8
  129.9 0.7 copy-start.9
  130.7 26.1 %all-to-all-start.2 = ((bf16[8,256,256]{2,1,0:T(8,128)(2,1)}), bf16[8,256,256]{2,1,0:T(8,128)(2,1)S(1)}, u32[]{:S(2)}, u32[]{:S(2)}) async-start(bf16[8,256,256]{2,1,0:T(8,128)(2,1)} %gate.1.refs_14_), calls=%async_computation.2 | async-start | bytes 2097152 | tf_op jit(solution)/shard_map/all_to_all | solution.py:672
  147.5 3.8 %collective-permute-start.17 = (bf16[256,256]{1,0:T(8,128)(2,1)}, bf16[256,256]{1,0:T(8,128)(2,1)S(1)}, u32[]{:S(2)}, u32[]{:S(2)}) collective-permute-start(bf16[256,256]{1,0:T(8,128)(2,1)} %get-tuple-element.60), channel_id=1, source_target_pairs={{0,4},{4,0},{8,12},{12,8},{16,20},{20,16},{24,28},{28,24},{1,5},{5... | collective-permute-start | bytes 393224 | tf_op jit(solution)/shard_map/ppermute | solution.py:665
  147.8 5.9 %collective-permute-start.18 = (bf16[256,256]{1,0:T(8,128)(2,1)}, bf16[256,256]{1,0:T(8,128)(2,1)S(1)}, u32[]{:S(2)}, u32[]{:S(2)}) collective-permute-start(bf16[256,256]{1,0:T(8,128)(2,1)} %get-tuple-element.61), channel_id=1, source_target_pairs={{0,8},{4,12},{8,0},{12,4},{16,24},{20,28},{24,16},{28,20},{1,9},{5... | collective-permute-start | bytes 393224 | tf_op jit(solution)/shard_map/ppermute | solution.py:665
  149.2 21.4 %collective-permute-start.19 = (bf16[256,256]{1,0:T(8,128)(2,1)}, bf16[256,256]{1,0:T(8,128)(2,1)S(1)}, u32[]{:S(2)}, u32[]{:S(2)}) collective-permute-start(bf16[256,256]{1,0:T(8,128)(2,1)} %get-tuple-element.62), channel_id=1, source_target_pairs={{0,12},{4,8},{8,4},{12,0},{16,28},{20,24},{24,20},{28,16},{1,13},{... | collective-permute-start | bytes 393224 | tf_op jit(solution)/shard_map/ppermute | solution.py:665
  149.8 20.9 %collective-permute-start.20 = (bf16[256,256]{1,0:T(8,128)(2,1)}, bf16[256,256]{1,0:T(8,128)(2,1)S(1)}, u32[]{:S(2)}, u32[]{:S(2)}) collective-permute-start(bf16[256,256]{1,0:T(8,128)(2,1)} %get-tuple-element.63), channel_id=1, source_target_pairs={{0,16},{4,20},{8,24},{12,28},{16,0},{20,4},{24,8},{28,12},{1,17},{... | collective-permute-start | bytes 393224 | tf_op jit(solution)/shard_map/ppermute | solution.py:665
  151.0 19.7 %collective-permute-start.21 = (bf16[256,256]{1,0:T(8,128)(2,1)}, bf16[256,256]{1,0:T(8,128)(2,1)S(1)}, u32[]{:S(2)}, u32[]{:S(2)}) collective-permute-start(bf16[256,256]{1,0:T(8,128)(2,1)} %get-tuple-element.64), channel_id=1, source_target_pairs={{0,20},{4,16},{8,28},{12,24},{16,4},{20,0},{24,12},{28,8},{1,21},{... | collective-permute-start | bytes 393224 | tf_op jit(solution)/shard_map/ppermute | solution.py:665
  151.3 16.3 %copy-start.13 = (bf16[256,256]{1,0:T(8,128)(2,1)}, bf16[256,256]{1,0:T(8,128)(2,1)S(1)}, u32[]{:S(2)}) copy-start(bf16[256,256]{1,0:T(8,128)(2,1)S(1)} %collective-permute-done.17.refs_1_) | copy-start | bytes 393220
  151.3 19.4 %collective-permute-start.22 = (bf16[256,256]{1,0:T(8,128)(2,1)}, bf16[256,256]{1,0:T(8,128)(2,1)S(1)}, u32[]{:S(2)}, u32[]{:S(2)}) collective-permute-start(bf16[256,256]{1,0:T(8,128)(2,1)} %get-tuple-element.65), channel_id=1, source_target_pairs={{0,24},{4,28},{8,16},{12,20},{16,8},{20,12},{24,0},{28,4},{1,25},{... | collective-permute-start | bytes 393224 | tf_op jit(solution)/shard_map/ppermute | solution.py:665
  153.7 14.0 %copy-start.14 = (bf16[256,256]{1,0:T(8,128)(2,1)}, bf16[256,256]{1,0:T(8,128)(2,1)S(1)}, u32[]{:S(2)}) copy-start(bf16[256,256]{1,0:T(8,128)(2,1)S(1)} %collective-permute-done.18.refs_2_) | copy-start | bytes 393220
  153.7 17.1 %collective-permute-start.23 = (bf16[256,256]{1,0:T(8,128)(2,1)}, bf16[256,256]{1,0:T(8,128)(2,1)S(1)}, u32[]{:S(2)}, u32[]{:S(2)}) collective-permute-start(bf16[256,256]{1,0:T(8,128)(2,1)} %get-tuple-element.66), channel_id=1, source_target_pairs={{0,28},{4,24},{8,20},{12,16},{16,12},{20,8},{24,4},{28,0},{1,29},{... | collective-permute-start | bytes 393224 | tf_op jit(solution)/shard_map/ppermute | solution.py:665
  156.7 1.0 copy-start
  170.7 0.6 copy-start.15
  170.7 0.7 copy-start.16
  170.7 0.7 copy-start.17
  170.7 0.8 copy-start.18
  170.7 0.8 copy-start.19

commit v3 on v1

--- a/solution.py
+++ b/solution.py
@@ -261,13 +261,17 @@
     select_ref[...] = jnp.where(token == own_ref[...], 1.0, 0.0).astype(BF16)
 
 
+def travel_order(shards):
+    return [0] + sorted(range(1, shards), key=lambda number: (number < 2, number & 1, number))
+
+
 def pack_kernel(shards, turn_ref, *refs):
     sources, outs = refs[: -shards - 3], refs[-shards - 3 : -3]
     held, in_sems, out_sems = refs[-3:]
     rows = sources[0].shape[0] // shards
 
     def read(number, place):
-        start = pl.multiple_of((turn_ref[0] ^ number) * rows, rows)
+        start = pl.multiple_of((turn_ref[0] ^ travel_order(shards)[number]) * rows, rows)
         return pltpu.make_async_copy(
             sources[place].at[pl.ds(start, rows)],
             held.at[number, pl.ds(place * rows, rows)],
@@ -394,7 +398,7 @@
             pltpu.VMEM(spec, BF16),
         ],
         compiler_params=params(),
-        cost_estimate=cost(6 * shards * rows * rows * width, 4 * filters.size + 8 * fh.size),
+        cost_estimate=cost(1e12, 1e9),
         name="filter_spectrum",
     )(filters, fh, fl, after)
 
@@ -572,14 +576,11 @@
     )(shared, a, b, after)
 
 
-def permuted(pieces):
-    shards = len(pieces)
-    order = sorted(range(1, shards), key=lambda number: (number < 2, number & 1, number))
-    received = {
-        number: lax.ppermute(pieces[number], "ctx", [(i, i ^ number) for i in range(shards)])
-        for number in order
-    }
-    return [pieces[0]] + [received[number] for number in range(1, shards)]
+def permuted(pieces, numbers):
+    return [pieces[0]] + [
+        lax.ppermute(piece, "ctx", [(i, i ^ number) for i in range(len(pieces))])
+        for piece, number in zip(pieces[1:], numbers[1:])
+    ]
 
 
 def exchange(value):
@@ -611,25 +612,27 @@
     grad_sources = (tensor_index - jnp.arange(tensor, dtype=jnp.int32)) % tensor
 
     both_packed = pack(turn, [key_rows, value_rows], shards)
-    both_slots = permuted(both_packed)
+    both_slots = permuted(both_packed, travel_order(shards))
     own = lax.dynamic_slice_in_dim(positions, ctx_index * slot_rows, slot_rows, 1)
     own_turned = jnp.concatenate(
-        [lax.dynamic_slice_in_dim(own, ctx_index ^ number, 1, 0) for number in range(shards)], axis=1
-    )
-
-    filter_spec = filter_spectrum(filters, tables, both_packed[0])
+        [lax.dynamic_slice_in_dim(own, ctx_index ^ number, 1, 0) for number in travel_order(shards)],
+        axis=1,
+    )
+
     grad_seq, query_seq, grad_conv = settle_query(
-        own.reshape(1, slots), query_recv, grad_sources, pieces, tokens, shards, [filter_spec]
-    )
-    grad_conv = gate(grad_conv, both_slots[1:])
+        own.reshape(1, slots), query_recv, grad_sources, pieces, tokens, shards, [both_packed[0]]
+    )
     grad_recv = exchange(grad_conv)
+    filter_spec = filter_spectrum(filters, tables, grad_conv)
+    grad_signal, grad_spec = convolve(
+        turn, [grad_recv], bias, filter_spec, tables, True, filter_spec
+    )
+    n_pieces = shards if (channels // shards) % 128 == 0 else 1
     key_seq, value_seq, signal = settle_signal(
-        turn, own_turned, both_slots, tokens, 1, grad_conv
-    )
-    signal_recv = [exchange(signal[0])]
-    grad_signal, grad_spec = convolve(
-        turn, [grad_recv], bias, filter_spec, tables, True, signal[0]
-    )
+        turn, own_turned, both_slots, tokens, n_pieces, grad_signal
+    )
+    signal_recv = permuted(signal, list(range(shards))) if n_pieces > 1 else [exchange(signal[0])]
+    grad_signal = gate(grad_signal, signal_recv)
     grad_signal_recv = exchange(grad_signal)
     conv_out, signal_spec = convolve(
         turn, signal_recv, bias, filter_spec, tables, False, grad_signal

time: 158 us -> 156 us (0.987)
  waiting for transfers between devices: 50.9 us -> 47.4 us
  starting transfers between devices: 30.4 us -> 32.2 us
    ppermute x7 -> x14, starting transfers between devices: 6.19 us -> 10.8 us  [permuted(): lax.ppermute(piece, 'ctx', [(i, i ^ number) for i in range(len(pieces))])]
    ppermute x7 -> x14, waiting for transfers between devices: 14.9 us -> 11.5 us  [permuted(): lax.ppermute(piece, 'ctx', [(i, i ^ number) for i in range(len(pieces))])]
    all_to_all x5 -> x4, starting transfers between devices: 19.6 us -> 16.9 us  [exchange(): return lax.all_to_all(value, 'ctx', split_axis=0, concat_axis=0, tiled=True)]
    all_to_all x5 -> x4, waiting for transfers between devices: 15.7 us -> 16.7 us  [exchange(): return lax.all_to_all(value, 'ctx', split_axis=0, concat_axis=0, tiled=True)]
  transfers between devices with their start and end apart: 15 -> 21, of which waited for: 10 -> 9; matrix products, arithmetic and copies ran while one was open for 3% -> 2% of each run, Pallas kernels for 42% -> 39%
where the time goes in v3:
time: 156 us; the launch traced here: 155 us
  Pallas kernels  68.7 us (44%)
  waiting for transfers between devices  47.4 us (30%)
  starting transfers between devices  32.2 us (21%)
  local copies, waits for them, and re-layouts  5.51 us (4%)
    pallas_call x2, Pallas kernels, convolve(): pl.pallas_call(functools.partial(conv_kernel, conjugate, scale, len(piece...  25.9 us
    ppermute x3, waiting for transfers between devices, per_device(): lax.ppermute(piece, 'tp', [(i, (i + shift) % tensor) for i in range(tenso...  19.1 us
    all_to_all x4, starting transfers between devices, exchange(): return lax.all_to_all(value, 'ctx', split_axis=0, concat_axis=0, tiled=True)  16.9 us
    all_to_all x4, waiting for transfers between devices, exchange(): return lax.all_to_all(value, 'ctx', split_axis=0, concat_axis=0, tiled=True)  16.7 us
    pallas_call x1, Pallas kernels, filter_spectrum(): pl.pallas_call(filter_kernel, grid=(shards,), in_specs=[whole(filters.sha...  12.3 us
    ppermute x14, waiting for transfers between devices, permuted(): lax.ppermute(piece, 'ctx', [(i, i ^ number) for i in range(len(pieces))])  11.5 us
    ppermute x14, starting transfers between devices, permuted(): lax.ppermute(piece, 'ctx', [(i, i ^ number) for i in range(len(pieces))])  10.8 us
    pallas_call x1, Pallas kernels, correlate(): pl.pallas_call(functools.partial(correlation_kernel, scale), grid=(shards...  10.6 us
  transfers between devices with their start and end apart: 21, of which 9 were waited for; matrix products, arithmetic and copies ran while one was open for 2% of the time, Pallas kernels for 39%

profile of v3, /device:TPU:0, one launch (start us, length us, event | category | flops | bytes accessed | tf_op | source)
XLA Modules:
  0.0 155.2 jit_solution(18058774166603120082)
XLA Ops:
  0.6 5.3 %all-to-all-start = ((bf16[8,64,2048]{2,1,0:T(8,128)(2,1)}), bf16[8,64,2048]{2,1,0:T(8,128)(2,1)S(1)}, u32[]{:S(2)}, u32[]{:S(2)}) async-start(bf16[8,64,2048]{2,1,0:T(8,128)(2,1)} %bitcast.5), calls=%async_computation | async-start | bytes 4194304 | tf_op jit(solution)/shard_map/all_to_all | solution.py:587
  6.0 3.7 %pack_rows.1 = (bf16[128,2048]{1,0:T(8,128)(2,1)}, bf16[128,2048]{1,0:T(8,128)(2,1)}, bf16[128,2048]{1,0:T(8,128)(2,1)}, bf16[128,2048]{1,0:T(8,128)(2,1)}, bf16...) custom-call(s32[1]{0:T(128)} %bitcast.turn_ref, ...), custom_call_target="tpu_custom_call" | custom-call | bytes 8388608 | tf_op jit(solution)/shard_map/pack_rows/pallas_call | solution.py:465
  9.6 2.1 %collective-permute-start.3 = (bf16[128,2048]{1,0:T(8,128)(2,1)}, bf16[128,2048]{1,0:T(8,128)(2,1)}, u32[]{:S(2)}, u32[]{:S(2)}) collective-permute-start(bf16[128,2048]{1,0:T(8,128)(2,1)} %get-tuple-element.37), channel_id=1, source_target_pairs={{0,8},{4,12},{8,0},{12,4},{16,24},{20,28},{24,16},{28,20},{1,9},{5... | collective-permute-start | bytes 1572872 | tf_op jit(solution)/shard_map/ppermute | solution.py:581
  11.7 1.5 collective-permute-start.4
  13.2 0.9 constant_dynamic-slice_fusion
  14.1 3.6 %collective-permute-start.2 = (bf16[64,2048]{1,0:T(8,128)(2,1)}, bf16[64,2048]{1,0:T(8,128)(2,1)S(1)}, u32[]{:S(2)}, u32[]{:S(2)}) collective-permute-start(bf16[64,2048]{1,0:T(8,128)(2,1)} %get-tuple-element.63), channel_id=1, source_target_pairs={{0,3},{1,0},{2,1},{3,2},{4,7},{5,4},{6,5},{7,6},{8,11},{9,8},{10,9... | collective-permute-start | bytes 786440 | tf_op jit(solution)/shard_map/ppermute | solution.py:610
  17.7 1.0 collective-permute-start.1
  18.7 0.1 constant_dynamic-slice_fusion.4
  18.8 0.7 reshape.22.own_ref
  19.4 0.1 fusion.1
  19.5 0.7 concatenate.3.own_ref
  20.2 0.6 and_select_fusion.source_ref
  20.8 4.0 %collective-permute-done.2.refs_3_ = bf16[64,2048]{1,0:T(8,128)(2,1)S(1)} collective-permute-done((bf16[64,2048]{1,0:T(8,128)(2,1)}, bf16[64,2048]{1,0:T(8,128)(2,1)S(1)}, u32[]{:S(2)}, u32[]{:S(2)}) %collective-permute-start.2) | collective-permute-done | bytes 262176 | tf_op jit(solution)/shard_map/ppermute | solution.py:610
  24.8 0.0 collective-permute-start.5
  24.8 6.5 %collective-permute-done.refs_1_ = bf16[64,2048]{1,0:T(8,128)(2,1)S(1)} collective-permute-done((bf16[64,2048]{1,0:T(8,128)(2,1)}, bf16[64,2048]{1,0:T(8,128)(2,1)S(1)}, u32[]{:S(2)}, u32[]{:S(2)}) %collective-permute-start) | collective-permute-done | bytes 262176 | tf_op jit(solution)/shard_map/ppermute | solution.py:610
  31.3 8.7 %collective-permute-done.1.refs_2_ = bf16[64,2048]{1,0:T(8,128)(2,1)S(1)} collective-permute-done((bf16[64,2048]{1,0:T(8,128)(2,1)S(1)}, bf16[64,2048]{1,0:T(8,128)(2,1)S(1)}, u32[]{:S(2)}, u32[]{:S(2)}) %collective-permute-start.1) | collective-permute-done | bytes 262176 | tf_op jit(solution)/shard_map/ppermute | solution.py:610
  40.0 0.0 copy-start
  40.0 0.7 copy-done.13
  40.7 0.7 copy-done
  41.4 4.6 %settle_query.1 = (bf16[256,2048]{1,0:T(8,128)(2,1)}, bf16[256,2048]{1,0:T(8,128)(2,1)}, bf16[8,256,256]{2,1,0:T(8,128)(2,1)}) custom-call(s32[4]{0:T(128)} %and_select_fusion.source_ref, s32[1,512]{1,0:T(1,128)} %reshape.22.own_ref, bf16[512,2048]{1,0:T(8,128)(2,1)} %bitcast.4, bf16[64,2048]{1,0:T(8,128)(2,1)} %get-tuple-element.65.refs_0_, ...), custom_call_target="tpu_custom_call" | custom-call | flops 536870912 | bytes 6291456 | tf_op jit(solution)/shard_map/settle_query/pallas_call | solution.py:545
  45.9 4.3 %all-to-all-start.1 = ((bf16[8,256,256]{2,1,0:T(8,128)(2,1)}), bf16[8,256,256]{2,1,0:T(8,128)(2,1)}, u32[]{:S(2)}, u32[]{:S(2)}) async-start(bf16[8,256,256]{2,1,0:T(8,128)(2,1)} %get-tuple-element.35.after_ref), calls=%async_computation.1 | async-start | bytes 2097152 | tf_op jit(solution)/shard_map/all_to_all | solution.py:587
  50.2 2.6 %collective-permute-start.8 = (bf16[128,2048]{1,0:T(8,128)(2,1)}, bf16[128,2048]{1,0:T(8,128)(2,1)}, u32[]{:S(2)}, u32[]{:S(2)}) collective-permute-start(bf16[128,2048]{1,0:T(8,128)(2,1)} %get-tuple-element.42), channel_id=1, source_target_pairs={{0,28},{4,24},{8,20},{12,16},{16,12},{20,8},{24,4},{28,0},{1,29},{... | collective-permute-start | bytes 1572872 | tf_op jit(solution)/shard_map/ppermute | solution.py:581
  52.8 0.4 collective-permute-start.9
  53.1 12.3 %filter_spectrum.1.refs_2_.refs_5_.refs_9_ = f32[8,512,256]{2,1,0:T(8,128)} custom-call(f32[256,2048]{1,0:T(8,128)} %filters_ref.1, bf16[8,512,512]{2,1,0:T(8,128)(2,1)} %constant.151.clone.fh_ref.refs_3_.refs_10_, bf16[8,512,512]{2,1,0:T(8,128)(2,1)} %constant.152.clone.fl_ref, bf16[8,256,256]{2,1,0:T(8,128)(2,1)} %get-tuple-element.35.after_ref), custom_call_target="tpu_custom_call" | custom-call | flops 999999995904 | bytes 1000000000 | tf_op jit(solution)/shard_map/filter_spectrum/pallas_call | solution.py:389
  65.4 12.8 %all-to-all-done.1.refs_0_ = bf16[8,256,256]{2,1,0:T(8,128)(2,1)} async-done(((bf16[8,256,256]{2,1,0:T(8,128)(2,1)}), bf16[8,256,256]{2,1,0:T(8,128)(2,1)}, u32[]{:S(2)}, u32[]{:S(2)}) %all-to-all-start.1) | async-done | bytes 1048608 | tf_op jit(solution)/shard_map/all_to_all | solution.py:587
  78.3 12.9 %convolve_backward.1 = (bf16[8,256,256]{2,1,0:T(8,128)(2,1)}, f32[8,512,256]{2,1,0:T(8,128)}) custom-call(s32[1]{0:T(128)} %bitcast.turn_ref, bf16[8,256,256]{2,1,0:T(8,128)(2,1)} %all-to-all-done.1.refs_0_, f32[1,256]{1,0:T(1,128)} %bitcast.6, f32[8,512,256]{2,1,0:T(8,128)} %filter_spectrum.1.refs_2_.refs_5_.refs_9_, ...), custom_call_target="tpu_custom_call" | custom-call | flops 2147483648 | bytes 20971520 | tf_op jit(solution)/shard_map/convolve_backward/pallas_call | solution.py:414
  91.2 5.7 %settle_signal.1 = (bf16[256,2048]{1,0:T(8,128)(2,1)}, bf16[256,2048]{1,0:T(8,128)(2,1)}, bf16[256,256]{1,0:T(8,128)(2,1)}, bf16[256,256]{1,0:T(8,128)(2,1)}, bf...) custom-call(s32[1]{0:T(128)} %bitcast.turn_ref, ...), custom_call_target="tpu_custom_call" | custom-call | flops 1073741824 | bytes 7340032 | tf_op jit(solution)/shard_map/settle_signal/pallas_call | solution.py:524
  96.9 0.1 collective-permute-start.10
  97.0 0.2 collective-permute-start.11
  97.2 1.6 %collective-permute-start.12 = (bf16[256,256]{1,0:T(8,128)(2,1)}, bf16[256,256]{1,0:T(8,128)(2,1)S(1)}, u32[]{:S(2)}, u32[]{:S(2)}) collective-permute-start(bf16[256,256]{1,0:T(8,128)(2,1)} %get-tuple-element.47), channel_id=1, source_target_pairs={{0,12},{4,8},{8,4},{12,0},{16,28},{20,24},{24,20},{28,16},{1,13},{... | collective-permute-start | bytes 393224 | tf_op jit(solution)/shard_map/ppermute | solution.py:581
  98.9 0.6 collective-permute-start.13
  99.4 1.1 collective-permute-start.14
  100.6 0.6 collective-permute-start.15
  101.2 2.4 %collective-permute-done.11.refs_3_.refs_2_ = bf16[256,256]{1,0:T(8,128)(2,1)S(1)} collective-permute-done((bf16[256,256]{1,0:T(8,128)(2,1)}, bf16[256,256]{1,0:T(8,128)(2,1)S(1)}, u32[]{:S(2)}, u32[]{:S(2)}) %collective-permute-start.11) | collective-permute-done | bytes 131104 | tf_op jit(solution)/shard_map/ppermute | solution.py:581
  103.6 1.9 %collective-permute-done.12.refs_4_.refs_3_ = bf16[256,256]{1,0:T(8,128)(2,1)S(1)} collective-permute-done((bf16[256,256]{1,0:T(8,128)(2,1)}, bf16[256,256]{1,0:T(8,128)(2,1)S(1)}, u32[]{:S(2)}, u32[]{:S(2)}) %collective-permute-start.12) | collective-permute-done | bytes 131104 | tf_op jit(solution)/shard_map/ppermute | solution.py:581
  105.5 7.2 %collective-permute-done.14.refs_6_.refs_5_ = bf16[256,256]{1,0:T(8,128)(2,1)S(1)} collective-permute-done((bf16[256,256]{1,0:T(8,128)(2,1)}, bf16[256,256]{1,0:T(8,128)(2,1)S(1)}, u32[]{:S(2)}, u32[]{:S(2)}) %collective-permute-start.14) | collective-permute-done | bytes 131104 | tf_op jit(solution)/shard_map/ppermute | solution.py:581
  112.7 0.6 copy-done.8
  113.3 0.1 copy-done.9
  113.4 0.0 copy-done.10
  113.4 3.7 %all-to-all-start.3 = ((bf16[8,256,256]{2,1,0:T(8,128)(2,1)}), bf16[8,256,256]{2,1,0:T(8,128)(2,1)S(1)}, u32[]{:S(2)}, u32[]{:S(2)}) async-start(bf16[8,256,256]{2,1,0:T(8,128)(2,1)} %gate.1.refs_12_), calls=%async_computation.3 | async-start | bytes 2097152 | tf_op jit(solution)/shard_map/all_to_all | solution.py:587
  117.2 13.0 %convolve_forward.1 = (bf16[8,256,256]{2,1,0:T(8,128)(2,1)}, f32[8,512,256]{2,1,0:T(8,128)}) custom-call(s32[1]{0:T(128)} %bitcast.turn_ref, bf16[256,256]{1,0:T(8,128)(2,1)} %get-tuple-element.44.refs_1_.refs_0_, bf16[256,256]{1,0:T(8,128)(2,1)} %copy-done.4, bf16[256,256]{1,0:T(8,128)(2,1)} %copy-done.5, bf16[256,256]{1,0:T(8,128)(2,1)} %copy-done.6, ...), custom_call_target="tpu_custom_call" | custom-call | flops 2147483648 | bytes 20971520 | tf_op jit(solution)/shard_map/convolve_forward/pallas_call | solution.py:414
  130.2 2.2 %all-to-all-done.3.shared_ref = bf16[8,256,256]{2,1,0:T(8,128)(2,1)S(1)} async-done(((bf16[8,256,256]{2,1,0:T(8,128)(2,1)}), bf16[8,256,256]{2,1,0:T(8,128)(2,1)S(1)}, u32[]{:S(2)}, u32[]{:S(2)}) %all-to-all-start.3) | async-done | bytes 1048608 | tf_op jit(solution)/shard_map/all_to_all | solution.py:587
  132.3 3.6 %all-to-all-start.2 = ((bf16[8,256,256]{2,1,0:T(8,128)(2,1)}), bf16[8,256,256]{2,1,0:T(8,128)(2,1)S(1)}, u32[]{:S(2)}, u32[]{:S(2)}) async-start(bf16[8,256,256]{2,1,0:T(8,128)(2,1)} %get-tuple-element.52), calls=%async_computation.2 | async-start | bytes 2097152 | tf_op jit(solution)/shard_map/all_to_all | solution.py:587
  135.9 10.6 %filter_gradient.1.after_ref = f32[256,2048]{1,0:T(8,128)} custom-call(f32[8,512,256]{2,1,0:T(8,128)} %get-tuple-element.57.spec_ref, f32[8,512,256]{2,1,0:T(8,128)} %get-tuple-element.58.other_ref, bf16[8,512,512]{2,1,0:T(8,128)(2,1)} %constant.153.clone.refs_4_.refs_11_.ih_ref), custom_call_target="tpu_custom_call" | custom-call | flops 2147483648 | bytes 16777216 | tf_op jit(solution)/shard_map/filter_gradient/pallas_call | solution.py:445
  146.5 3.0 %key_value_gradients.1 = (bf16[256,2048]{1,0:T(8,128)(2,1)}, bf16[256,2048]{1,0:T(8,128)(2,1)}) custom-call(bf16[8,256,256]{2,1,0:T(8,128)(2,1)} %copy-done.1, bf16[256,2048]{1,0:T(8,128)(2,1)} %get-tuple-element.55.a_ref, bf16[256,2048]{1,0:T(8,128)(2,1)} %get-tuple-element.56.b_ref, f32[256,2048]{1,0:T(8,128)} %filter_gradient.1.after_ref), custom_call_target="tpu_custom_call" | custom-call | flops 1048576 | bytes 5242880 | tf_op jit(solution)/shard_map/key_value_gradients/pallas_call | solution.py:564
  149.5 1.7 %all-to-all-done.2.shared_ref = bf16[8,256,256]{2,1,0:T(8,128)(2,1)S(1)} async-done(((bf16[8,256,256]{2,1,0:T(8,128)(2,1)}), bf16[8,256,256]{2,1,0:T(8,128)(2,1)S(1)}, u32[]{:S(2)}, u32[]{:S(2)}) %all-to-all-start.2) | async-done | bytes 1048608 | tf_op jit(solution)/shard_map/all_to_all | solution.py:587
  151.2 1.0 copy-done.2
  152.2 3.0 %output_and_query_gradient.1 = (bf16[256,2048]{1,0:T(8,128)(2,1)}, bf16[256,2048]{1,0:T(8,128)(2,1)}) custom-call(bf16[8,256,256]{2,1,0:T(8,128)(2,1)} %copy-done.2, bf16[256,2048]{1,0:T(8,128)(2,1)} %get-tuple-element.53.a_ref, bf16[256,2048]{1,0:T(8,128)(2,1)} %get-tuple-element.54.b_ref, bf16[256,2048]{1,0:T(8,128)(2,1)} %get-tuple-element.31.after_ref), custom_call_target="tpu_custom_call" | custom-call | flops 1048576 | bytes 5242880 | tf_op jit(solution)/shard_map/output_and_query_gradient/pallas_call | solution.py:564
  (40 shorter events, 0.1 us)
Async XLA Ops:
  0.6 12.6 %copy-start.3 = (bf16[64,8192]{1,0:T(8,128)(2,1)S(1)}, bf16[64,8192]{1,0:T(8,128)(2,1)}, u32[]{:S(2)}) copy-start(bf16[64,8192]{1,0:T(8,128)(2,1)} %param.16) | copy-start | bytes 3145732
  0.6 39.3 %all-to-all-start = ((bf16[8,64,2048]{2,1,0:T(8,128)(2,1)}), bf16[8,64,2048]{2,1,0:T(8,128)(2,1)S(1)}, u32[]{:S(2)}, u32[]{:S(2)}) async-start(bf16[8,64,2048]{2,1,0:T(8,128)(2,1)} %bitcast.5), calls=%async_computation | async-start | bytes 4194304 | tf_op jit(solution)/shard_map/all_to_all | solution.py:587
  6.0 12.8 %copy-start.14 = (s32[8,512]{1,0:T(8,128)S(1)}, s32[8,512]{1,0:T(8,128)}, u32[]{:S(2)}) copy-start(s32[8,512]{1,0:T(8,128)} %param.13) | copy-start | bytes 49156
  9.6 40.6 %collective-permute-start.3 = (bf16[128,2048]{1,0:T(8,128)(2,1)}, bf16[128,2048]{1,0:T(8,128)(2,1)}, u32[]{:S(2)}, u32[]{:S(2)}) collective-permute-start(bf16[128,2048]{1,0:T(8,128)(2,1)} %get-tuple-element.37), channel_id=1, source_target_pairs={{0,8},{4,12},{8,0},{12,4},{16,24},{20,28},{24,16},{28,20},{1,9},{5... | collective-permute-start | bytes 1572872 | tf_op jit(solution)/shard_map/ppermute | solution.py:581
  11.7 41.1 %collective-permute-start.4 = (bf16[128,2048]{1,0:T(8,128)(2,1)}, bf16[128,2048]{1,0:T(8,128)(2,1)}, u32[]{:S(2)}, u32[]{:S(2)}) collective-permute-start(bf16[128,2048]{1,0:T(8,128)(2,1)} %get-tuple-element.38), channel_id=1, source_target_pairs={{0,16},{4,20},{8,24},{12,28},{16,0},{20,4},{24,8},{28,12},{1,17},{... | collective-permute-start | bytes 1572872 | tf_op jit(solution)/shard_map/ppermute | solution.py:581
  14.1 10.7 %collective-permute-start.2 = (bf16[64,2048]{1,0:T(8,128)(2,1)}, bf16[64,2048]{1,0:T(8,128)(2,1)S(1)}, u32[]{:S(2)}, u32[]{:S(2)}) collective-permute-start(bf16[64,2048]{1,0:T(8,128)(2,1)} %get-tuple-element.63), channel_id=1, source_target_pairs={{0,3},{1,0},{2,1},{3,2},{4,7},{5,4},{6,5},{7,6},{8,11},{9,8},{10,9... | collective-permute-start | bytes 786440 | tf_op jit(solution)/shard_map/ppermute | solution.py:610
  17.7 13.6 %collective-permute-start = (bf16[64,2048]{1,0:T(8,128)(2,1)}, bf16[64,2048]{1,0:T(8,128)(2,1)S(1)}, u32[]{:S(2)}, u32[]{:S(2)}) collective-permute-start(bf16[64,2048]{1,0:T(8,128)(2,1)} %get-tuple-element.64), channel_id=1, source_target_pairs={{0,1},{1,2},{2,3},{3,0},{4,5},{5,6},{6,7},{7,4},{8,9},{9,10},{10,1... | collective-permute-start | bytes 786440 | tf_op jit(solution)/shard_map/ppermute | solution.py:610
  17.7 22.3 %collective-permute-start.1 = (bf16[64,2048]{1,0:T(8,128)(2,1)S(1)}, bf16[64,2048]{1,0:T(8,128)(2,1)S(1)}, u32[]{:S(2)}, u32[]{:S(2)}) collective-permute-start(bf16[64,2048]{1,0:T(8,128)(2,1)S(1)} %get-tuple-element.66), channel_id=1, source_target_pairs={{0,2},{1,3},{2,0},{3,1},{4,6},{5,7},{6,4},{7,5},{8,10},{9,11},{10,... | collective-permute-start | bytes 786440 | tf_op jit(solution)/shard_map/ppermute | solution.py:610
  24.8 15.2 %copy-start.11 = (bf16[64,2048]{1,0:T(8,128)(2,1)}, bf16[64,2048]{1,0:T(8,128)(2,1)S(1)}, u32[]{:S(2)}) copy-start(bf16[64,2048]{1,0:T(8,128)(2,1)S(1)} %collective-permute-done.2.refs_3_) | copy-start | bytes 786436
  24.8 66.4 %collective-permute-start.5 = (bf16[128,2048]{1,0:T(8,128)(2,1)}, bf16[128,2048]{1,0:T(8,128)(2,1)}, u32[]{:S(2)}, u32[]{:S(2)}) collective-permute-start(bf16[128,2048]{1,0:T(8,128)(2,1)} %get-tuple-element.39), channel_id=1, source_target_pairs={{0,24},{4,28},{8,16},{12,20},{16,8},{20,12},{24,0},{28,4},{1,25},{... | collective-permute-start | bytes 1572872 | tf_op jit(solution)/shard_map/ppermute | solution.py:581
  31.3 8.7 %copy-start.12 = (bf16[64,2048]{1,0:T(8,128)(2,1)}, bf16[64,2048]{1,0:T(8,128)(2,1)S(1)}, u32[]{:S(2)}) copy-start(bf16[64,2048]{1,0:T(8,128)(2,1)S(1)} %collective-permute-done.refs_1_) | copy-start | bytes 786436
  31.3 59.9 %collective-permute-start.6 = (bf16[128,2048]{1,0:T(8,128)(2,1)}, bf16[128,2048]{1,0:T(8,128)(2,1)}, u32[]{:S(2)}, u32[]{:S(2)}) collective-permute-start(bf16[128,2048]{1,0:T(8,128)(2,1)} %get-tuple-element.40), channel_id=1, source_target_pairs={{0,12},{4,8},{8,4},{12,0},{16,28},{20,24},{24,20},{28,16},{1,13},{... | collective-permute-start | bytes 1572872 | tf_op jit(solution)/shard_map/ppermute | solution.py:581
  40.0 0.7 copy-start.13
  40.0 51.2 %collective-permute-start.7 = (bf16[128,2048]{1,0:T(8,128)(2,1)}, bf16[128,2048]{1,0:T(8,128)(2,1)}, u32[]{:S(2)}, u32[]{:S(2)}) collective-permute-start(bf16[128,2048]{1,0:T(8,128)(2,1)} %get-tuple-element.41), channel_id=1, source_target_pairs={{0,20},{4,16},{8,28},{12,24},{16,4},{20,0},{24,12},{28,8},{1,21},{... | collective-permute-start | bytes 1572872 | tf_op jit(solution)/shard_map/ppermute | solution.py:581
  40.0 1.4 copy-start
  45.9 32.3 %all-to-all-start.1 = ((bf16[8,256,256]{2,1,0:T(8,128)(2,1)}), bf16[8,256,256]{2,1,0:T(8,128)(2,1)}, u32[]{:S(2)}, u32[]{:S(2)}) async-start(bf16[8,256,256]{2,1,0:T(8,128)(2,1)} %get-tuple-element.35.after_ref), calls=%async_computation.1 | async-start | bytes 2097152 | tf_op jit(solution)/shard_map/all_to_all | solution.py:587
  50.2 41.0 %collective-permute-start.8 = (bf16[128,2048]{1,0:T(8,128)(2,1)}, bf16[128,2048]{1,0:T(8,128)(2,1)}, u32[]{:S(2)}, u32[]{:S(2)}) collective-permute-start(bf16[128,2048]{1,0:T(8,128)(2,1)} %get-tuple-element.42), channel_id=1, source_target_pairs={{0,28},{4,24},{8,20},{12,16},{16,12},{20,8},{24,4},{28,0},{1,29},{... | collective-permute-start | bytes 1572872 | tf_op jit(solution)/shard_map/ppermute | solution.py:581
  52.8 38.4 %collective-permute-start.9 = (bf16[128,2048]{1,0:T(8,128)(2,1)}, bf16[128,2048]{1,0:T(8,128)(2,1)}, u32[]{:S(2)}, u32[]{:S(2)}) collective-permute-start(bf16[128,2048]{1,0:T(8,128)(2,1)} %get-tuple-element.43), channel_id=1, source_target_pairs={{0,4},{4,0},{8,12},{12,8},{16,20},{20,16},{24,28},{28,24},{1,5},{5... | collective-permute-start | bytes 1572872 | tf_op jit(solution)/shard_map/ppermute | solution.py:581
  96.9 3.6 %collective-permute-start.10 = (bf16[256,256]{1,0:T(8,128)(2,1)}, bf16[256,256]{1,0:T(8,128)(2,1)S(1)}, u32[]{:S(2)}, u32[]{:S(2)}) collective-permute-start(bf16[256,256]{1,0:T(8,128)(2,1)} %get-tuple-element.45), channel_id=1, source_target_pairs={{0,4},{4,0},{8,12},{12,8},{16,20},{20,16},{24,28},{28,24},{1,5},{5... | collective-permute-start | bytes 393224 | tf_op jit(solution)/shard_map/ppermute | solution.py:581
  97.0 6.6 %collective-permute-start.11 = (bf16[256,256]{1,0:T(8,128)(2,1)}, bf16[256,256]{1,0:T(8,128)(2,1)S(1)}, u32[]{:S(2)}, u32[]{:S(2)}) collective-permute-start(bf16[256,256]{1,0:T(8,128)(2,1)} %get-tuple-element.46), channel_id=1, source_target_pairs={{0,8},{4,12},{8,0},{12,4},{16,24},{20,28},{24,16},{28,20},{1,9},{5... | collective-permute-start | bytes 393224 | tf_op jit(solution)/shard_map/ppermute | solution.py:581
  97.2 8.2 %collective-permute-start.12 = (bf16[256,256]{1,0:T(8,128)(2,1)}, bf16[256,256]{1,0:T(8,128)(2,1)S(1)}, u32[]{:S(2)}, u32[]{:S(2)}) collective-permute-start(bf16[256,256]{1,0:T(8,128)(2,1)} %get-tuple-element.47), channel_id=1, source_target_pairs={{0,12},{4,8},{8,4},{12,0},{16,28},{20,24},{24,20},{28,16},{1,13},{... | collective-permute-start | bytes 393224 | tf_op jit(solution)/shard_map/ppermute | solution.py:581
  98.9 6.6 %collective-permute-start.13 = (bf16[256,256]{1,0:T(8,128)(2,1)}, bf16[256,256]{1,0:T(8,128)(2,1)S(1)}, u32[]{:S(2)}, u32[]{:S(2)}) collective-permute-start(bf16[256,256]{1,0:T(8,128)(2,1)} %get-tuple-element.48), channel_id=1, source_target_pairs={{0,16},{4,20},{8,24},{12,28},{16,0},{20,4},{24,8},{28,12},{1,17},{... | collective-permute-start | bytes 393224 | tf_op jit(solution)/shard_map/ppermute | solution.py:581
  99.4 13.2 %collective-permute-start.14 = (bf16[256,256]{1,0:T(8,128)(2,1)}, bf16[256,256]{1,0:T(8,128)(2,1)S(1)}, u32[]{:S(2)}, u32[]{:S(2)}) collective-permute-start(bf16[256,256]{1,0:T(8,128)(2,1)} %get-tuple-element.49), channel_id=1, source_target_pairs={{0,20},{4,16},{8,28},{12,24},{16,4},{20,0},{24,12},{28,8},{1,21},{... | collective-permute-start | bytes 393224 | tf_op jit(solution)/shard_map/ppermute | solution.py:581
  100.6 12.1 %copy-start.4 = (bf16[256,256]{1,0:T(8,128)(2,1)}, bf16[256,256]{1,0:T(8,128)(2,1)S(1)}, u32[]{:S(2)}) copy-start(bf16[256,256]{1,0:T(8,128)(2,1)S(1)} %collective-permute-done.10.refs_2_.refs_1_) | copy-start | bytes 393220
  100.6 12.1 %collective-permute-start.15 = (bf16[256,256]{1,0:T(8,128)(2,1)}, bf16[256,256]{1,0:T(8,128)(2,1)S(1)}, u32[]{:S(2)}, u32[]{:S(2)}) collective-permute-start(bf16[256,256]{1,0:T(8,128)(2,1)} %get-tuple-element.50), channel_id=1, source_target_pairs={{0,24},{4,28},{8,16},{12,20},{16,8},{20,12},{24,0},{28,4},{1,25},{... | collective-permute-start | bytes 393224 | tf_op jit(solution)/shard_map/ppermute | solution.py:581
  103.6 9.1 %copy-start.5 = (bf16[256,256]{1,0:T(8,128)(2,1)}, bf16[256,256]{1,0:T(8,128)(2,1)S(1)}, u32[]{:S(2)}) copy-start(bf16[256,256]{1,0:T(8,128)(2,1)S(1)} %collective-permute-done.11.refs_3_.refs_2_) | copy-start | bytes 393220
  103.6 9.1 %collective-permute-start.16 = (bf16[256,256]{1,0:T(8,128)(2,1)}, bf16[256,256]{1,0:T(8,128)(2,1)S(1)}, u32[]{:S(2)}, u32[]{:S(2)}) collective-permute-start(bf16[256,256]{1,0:T(8,128)(2,1)} %get-tuple-element.51), channel_id=1, source_target_pairs={{0,28},{4,24},{8,20},{12,16},{16,12},{20,8},{24,4},{28,0},{1,29},{... | collective-permute-start | bytes 393224 | tf_op jit(solution)/shard_map/ppermute | solution.py:581
  105.5 7.2 %copy-start.6 = (bf16[256,256]{1,0:T(8,128)(2,1)}, bf16[256,256]{1,0:T(8,128)(2,1)S(1)}, u32[]{:S(2)}) copy-start(bf16[256,256]{1,0:T(8,128)(2,1)S(1)} %collective-permute-done.12.refs_4_.refs_3_) | copy-start | bytes 393220
  105.5 7.2 %copy-start.7 = (bf16[256,256]{1,0:T(8,128)(2,1)}, bf16[256,256]{1,0:T(8,128)(2,1)S(1)}, u32[]{:S(2)}) copy-start(bf16[256,256]{1,0:T(8,128)(2,1)S(1)} %collective-permute-done.13.refs_5_.refs_4_) | copy-start | bytes 393220
  112.7 0.7 copy-start.8
  112.7 0.7 copy-start.9
  112.7 0.7 copy-start.10
  113.4 18.9 %all-to-all-start.3 = ((bf16[8,256,256]{2,1,0:T(8,128)(2,1)}), bf16[8,256,256]{2,1,0:T(8,128)(2,1)S(1)}, u32[]{:S(2)}, u32[]{:S(2)}) async-start(bf16[8,256,256]{2,1,0:T(8,128)(2,1)} %gate.1.refs_12_), calls=%async_computation.3 | async-start | bytes 2097152 | tf_op jit(solution)/shard_map/all_to_all | solution.py:587
  132.3 14.2 %copy-start.1 = (bf16[8,256,256]{2,1,0:T(8,128)(2,1)}, bf16[8,256,256]{2,1,0:T(8,128)(2,1)S(1)}, u32[]{:S(2)}) copy-start(bf16[8,256,256]{2,1,0:T(8,128)(2,1)S(1)} %all-to-all-done.3.shared_ref) | copy-start | bytes 3145732
  132.3 18.9 %all-to-all-start.2 = ((bf16[8,256,256]{2,1,0:T(8,128)(2,1)}), bf16[8,256,256]{2,1,0:T(8,128)(2,1)S(1)}, u32[]{:S(2)}, u32[]{:S(2)}) async-start(bf16[8,256,256]{2,1,0:T(8,128)(2,1)} %get-tuple-element.52), calls=%async_computation.2 | async-start | bytes 2097152 | tf_op jit(solution)/shard_map/all_to_all | solution.py:587
  151.2 1.0 copy-start.2
